TPU v7x, 32 devices: a whole 2x2x4 slice. The times are simulated.
32 devices in a mesh: req: 8 (over y, x, core), mdl: 4 (over z).
Axes of the slice: x: 2, y: 2, z: 4, core: 2. Of those that a mesh axis runs over, the one named last changes fastest.
Arguments:
- hidden_in: bfloat16 [64, 16, 2048], P('req'), may hold values from -6 to 6
- mixer_gain: bfloat16 [2048], replicated, may hold values from 0.5 to 1.5
- w_query: bfloat16 [2048, 1024], P(None, 'mdl'), may hold values from -0.125 to 0.125
- w_kv: bfloat16 [2, 2048, 256], replicated, may hold values from -0.125 to 0.125
- w_attn_out: bfloat16 [1024, 2048], P('mdl'), may hold values from -0.1875 to 0.1875
- prompt_kv: bfloat16 [16, 2, 1024, 256], P('req')
- prompt_lengths: int32 [16], P('req'), may hold values from 1 to 1024, as said below
- member: int32 [64], P('req'), may hold values from 0 to 1
- accepted: int32 [64], P('req'), may hold values from 1 to 16, as said below
- w_z: bfloat16 [2048, 1536], P(None, 'mdl'), may hold values from -0.125 to 0.125
- w_x: bfloat16 [2048, 1536], P(None, 'mdl'), may hold values from -0.125 to 0.125
- w_bc: bfloat16 [2048, 512], replicated, may hold values from -0.125 to 0.125
- w_dt: bfloat16 [2048, 24], P(None, 'mdl'), may hold values from -0.125 to 0.125
- conv_x: bfloat16 [4, 1536], P(None, 'mdl'), may hold values from -1.5 to 1.5
- conv_bc: bfloat16 [4, 512], replicated, may hold values from -1.5 to 1.5
- ssm_rate: float32 [24], P('mdl'), may hold values from 1 to 16
- dt_bias: float32 [24], P('mdl'), may hold values from -4 to 0.5
- skip_d: float32 [24], P('mdl'), may hold values from 0.5 to 1.5
- prompt_state: float32 [16, 24, 64, 256], P('req', 'mdl'), may hold values from -0.4 to 0.4
- prompt_conv_x: bfloat16 [16, 3, 1536], P('req', None, 'mdl'), may hold values from -6 to 6
- prompt_conv_bc: bfloat16 [16, 3, 512], P('req'), may hold values from -6 to 6
- w_mamba_out: bfloat16 [1536, 2048], P('mdl'), may hold values from -0.15625 to 0.15625
- mlp_gain: bfloat16 [2048], replicated, may hold values from 0.5 to 1.5
- w_gate: bfloat16 [2048, 4096], P(None, 'req'), may hold values from -0.125 to 0.125
- w_up: bfloat16 [2048, 4096], P(None, 'req'), may hold values from -0.125 to 0.125
- w_down: bfloat16 [4096, 2048], P('req'), may hold values from -0.09375 to 0.09375
- final_gain: bfloat16 [2048], replicated, may hold values from 0.5 to 1.5
- head_weight: bfloat16 [32768, 2048], P('req')
- draft_ids: int32 [64, 16], replicated, may hold values from 0 to 32767
Outputs:
- hidden_out: bfloat16 [64, 16, 2048], P(('req', 'mdl'))
- verify_scores: float32 [64, 16], P(('req', 'mdl'))
- kept_state: float32 [64, 24, 64, 256], P(('req', 'mdl'))
- kept_conv: bfloat16 [64, 3, 2048], P(('req', 'mdl'))
Inputs may be any that keep to these rules, and one draw needn't show every extreme that they name: Each request has accepted 1 to 16 drafts; both ends occur in every draw. `prompt_lengths`: a prompt of 1024 tokens occurs in every draw. `member`: index of the request's prompt among the 2 prompts of its block of 8 requests.
All inputs are finite; a program needn't handle non-finite values.
Results may differ from a plain program's by a relative error of at most 0.017.
Values may be sent and summed in bfloat16 or wider, within the bound.
A program may use at most 128 MiB of HBM per device.

v0:
```python
import jax
import jax.numpy as jnp
from jax import lax
from jax.sharding import PartitionSpec as P

Q_HEADS = 8
KV_HEADS = 2
HEAD_DIM = 128
SSM_DIM = 64
STATE = 256
CONV = 4
PROMPTS = 2
P_MAX = 1024


eps_norm = 1e-05
far_below = -1e30


def joined_2(part, axis, combine):
    gathered = jax.tree.map(lambda a: lax.all_gather(a, axis), part)

    def take(source):
        return jax.tree.map(lambda a: lax.dynamic_index_in_dim(a, source, 0, False), gathered)

    return lax.fori_loop(
        1, lax.axis_size(axis), lambda source, state: combine(state, take(source)), take(0)
    )


def rms_scale(values, gain):
    widened = values.astype(jnp.float32)
    spread = jnp.mean(widened * widened, axis=-1, keepdims=True)
    return widened * lax.rsqrt(spread + eps_norm) * gain.astype(jnp.float32)


def convolve(series, kernel, length):
    summed = jnp.zeros(series.shape[:-2] + (length, series.shape[-1]), jnp.float32)
    for kernel_tap in range(kernel.shape[0]):
        window = lax.slice_in_dim(series, kernel_tap, kernel_tap + length, axis=series.ndim - 2)
        summed = summed + window * kernel[kernel_tap].astype(jnp.float32)
    return jax.nn.silu(summed)


def combine_stats(first, second):
    joint_top = jnp.maximum(first[0], second[0])
    joint_total = first[1] * jnp.exp(first[0] - joint_top) + second[1] * jnp.exp(
        second[0] - joint_top
    )
    return (joint_top, joint_total, first[2] + second[2])


def shards(
    hidden_in,
    mixer_gain,
    w_query,
    w_kv,
    w_attn_out,
    prompt_kv,
    prompt_lengths,
    member,
    accepted,
    w_z,
    w_x,
    w_bc,
    w_dt,
    conv_x,
    conv_bc,
    ssm_rate,
    dt_bias,
    skip_d,
    prompt_state,
    prompt_conv_x,
    prompt_conv_bc,
    w_mamba_out,
    mlp_gain,
    w_gate,
    w_up,
    w_down,
    final_gain,
    head_weight,
    draft_ids,
):
    row_reqs, draft_len, width = hidden_in.shape
    mdl_count = lax.axis_size("mdl")
    req_count = lax.axis_size("req")
    mdl_rank = lax.axis_index("mdl")
    req_rank = lax.axis_index("req")
    row_tokens = row_reqs * draft_len
    own_reqs = row_reqs // mdl_count
    own_tokens = own_reqs * draft_len
    contract_last = (((1,), (1,)), ((), ()))
    flat_rows = hidden_in.reshape(row_tokens, width)
    normed = rms_scale(flat_rows, mixer_gain).astype(jnp.bfloat16)
    token_request = jnp.arange(row_tokens) // draft_len
    token_position = jnp.arange(row_tokens) % draft_len
    prompt_pick = jax.nn.one_hot(member, PROMPTS, dtype=jnp.float32)
    local_heads = w_query.shape[1] // HEAD_DIM
    per_group = Q_HEADS // KV_HEADS
    kv_index = mdl_rank * local_heads // per_group
    kv_weight = lax.dynamic_index_in_dim(w_kv, kv_index, 0, keepdims=False)
    queries = jnp.dot(normed, w_query, preferred_element_type=jnp.float32).astype(jnp.bfloat16)
    key_value = jnp.dot(normed, kv_weight, preferred_element_type=jnp.float32).astype(jnp.bfloat16)
    draft_keys = key_value[:, :HEAD_DIM]
    draft_values = key_value[:, HEAD_DIM:]
    query_rows = (
        queries.reshape(row_tokens, local_heads, HEAD_DIM)
        .transpose(1, 0, 2)
        .reshape(local_heads * row_tokens, HEAD_DIM)
    )
    row_request = jnp.tile(token_request, local_heads)
    row_position = jnp.tile(token_position, local_heads)
    row_member = jnp.take(member, row_request)
    cached = lax.dynamic_index_in_dim(prompt_kv, kv_index, 1, keepdims=False)
    score_scale = HEAD_DIM ** (-0.5)
    draft_scores = (
        lax.dot_general(query_rows, draft_keys, contract_last, preferred_element_type=jnp.float32)
        * score_scale
    )
    draft_mask = (row_request[:, None] == token_request[None, :]) & (
        token_position[None, :] <= row_position[:, None]
    )
    draft_top = jnp.max(jnp.where(draft_mask, draft_scores, far_below), axis=1)

    def prompt_scores(prompt_slot, row_count):
        key_block = cached[prompt_slot]
        scores = (
            lax.dot_general(
                query_rows,
                key_block[:, :HEAD_DIM],
                contract_last,
                preferred_element_type=jnp.float32,
            )
            * score_scale
        )
        positions = jnp.arange(row_count)
        valid_keys = (row_member[:, None] == prompt_slot) & (
            positions[None, :] < prompt_lengths[prompt_slot]
        )
        return (scores, valid_keys, key_block[:, HEAD_DIM:])

    def add_weights(carry, scores, valid_keys, values_block, row_top):
        weight_total, weighted = carry
        weights = jnp.exp(jnp.where(valid_keys, scores - row_top[:, None], far_below))
        weight_total = weight_total + jnp.sum(weights, axis=1)
        weighted = weighted + jnp.dot(
            weights.astype(jnp.bfloat16), values_block, preferred_element_type=jnp.float32
        )
        return (weight_total, weighted)

    row_top = draft_top
    prompt_parts = []
    for prompt_slot in range(PROMPTS):
        scores, valid_keys, values_block = prompt_scores(prompt_slot, P_MAX)
        row_top = jnp.maximum(row_top, jnp.max(jnp.where(valid_keys, scores, far_below), axis=1))
        prompt_parts.append((scores, valid_keys, values_block))
    carry = (
        jnp.zeros(row_top.shape, jnp.float32),
        jnp.zeros((query_rows.shape[0], HEAD_DIM), jnp.float32),
    )
    for scores, valid_keys, values_block in prompt_parts:
        carry = add_weights(carry, scores, valid_keys, values_block, row_top)
    carry = add_weights(carry, draft_scores, draft_mask, draft_values, row_top)
    attended = (carry[1] / carry[0][:, None]).astype(jnp.bfloat16)
    attention_flat = (
        attended.reshape(local_heads, row_tokens, HEAD_DIM)
        .transpose(1, 0, 2)
        .reshape(row_tokens, local_heads * HEAD_DIM)
    )
    gate_z = jnp.dot(normed, w_z, preferred_element_type=jnp.float32).astype(jnp.bfloat16)
    ssm_in = jnp.dot(normed, w_x, preferred_element_type=jnp.float32).astype(jnp.bfloat16)
    bc_in = jnp.dot(normed, w_bc, preferred_element_type=jnp.float32).astype(jnp.bfloat16)
    dt_in = jnp.dot(normed, w_dt, preferred_element_type=jnp.float32).astype(jnp.bfloat16)
    local_inner = w_x.shape[1]
    local_ssm = local_inner // SSM_DIM
    edge_len = CONV - 1
    start_x = jnp.einsum(
        "rp,pcw->rcw",
        prompt_pick,
        prompt_conv_x.astype(jnp.float32),
        precision=lax.Precision.HIGHEST,
    )
    start_bc = jnp.einsum(
        "rp,pcw->rcw",
        prompt_pick,
        prompt_conv_bc.astype(jnp.float32),
        precision=lax.Precision.HIGHEST,
    )
    series_x = jnp.concatenate(
        [start_x, ssm_in.astype(jnp.float32).reshape(row_reqs, draft_len, local_inner)], axis=1
    )
    series_bc = jnp.concatenate(
        [start_bc, bc_in.astype(jnp.float32).reshape(row_reqs, draft_len, 2 * STATE)], axis=1
    )
    conv_xs = convolve(series_x, conv_x, draft_len)
    conv_bcs = convolve(series_bc, conv_bc, draft_len)
    b_part = conv_bcs[:, :, :STATE]
    c_part = conv_bcs[:, :, STATE:]
    step_size = jax.nn.softplus(
        dt_in.astype(jnp.float32).reshape(row_reqs, draft_len, local_ssm) + dt_bias
    )
    log_decay = jnp.cumsum(-step_size * ssm_rate, axis=1)
    heads_x = conv_xs.reshape(row_reqs, draft_len, local_ssm, SSM_DIM)
    causal_pairs = jnp.arange(draft_len)[:, None] >= jnp.arange(draft_len)[None, :]
    log_gaps = log_decay[:, :, None, :] - log_decay[:, None, :, :]
    mixing = jnp.exp(jnp.where(causal_pairs[None, :, :, None], log_gaps, far_below))
    intersection = jnp.einsum("rtn,rsn->rts", c_part, b_part, precision=lax.Precision.HIGHEST)
    pair_weights = mixing * intersection[..., None] * step_size[:, None, :, :]
    intra = jnp.einsum("rtsh,rshp->rthp", pair_weights, heads_x, precision=lax.Precision.HIGHEST)
    initial = jnp.einsum(
        "rp,phdn->rhdn", prompt_pick, prompt_state, precision=lax.Precision.HIGHEST
    )
    carried = (
        jnp.einsum("rhdn,rtn->rthd", initial, c_part, precision=lax.Precision.HIGHEST)
        * jnp.exp(log_decay)[..., None]
    )
    ssm_out = intra + carried + skip_d[None, None, :, None] * heads_x
    gated = (
        ssm_out.reshape(row_tokens, local_inner) * jax.nn.silu(gate_z.astype(jnp.float32))
    ).astype(jnp.bfloat16)
    last_index = accepted - 1
    pick_step = jax.nn.one_hot(last_index, draft_len, dtype=jnp.float32)
    final_log = jnp.einsum("rt,rth->rh", pick_step, log_decay, precision=lax.Precision.HIGHEST)
    upto_last = jnp.arange(draft_len)[None, :] <= last_index[:, None]
    carry_weights = (
        jnp.exp(jnp.where(upto_last[:, :, None], final_log[:, None, :] - log_decay, far_below))
        * step_size
    )
    kept_states = jnp.exp(final_log)[:, :, None, None] * initial
    kept_states = kept_states + jnp.einsum(
        "rsh,rshd,rsn->rhdn", carry_weights, heads_x, b_part, precision=lax.Precision.HIGHEST
    )
    window_pick = jax.nn.one_hot(
        accepted[:, None] + jnp.arange(edge_len)[None, :], edge_len + draft_len, dtype=jnp.float32
    )
    kept_x = jnp.einsum("rkl,rlc->rkc", window_pick, series_x, precision=lax.Precision.HIGHEST)
    kept_bc = jnp.einsum("rkl,rlc->rkc", window_pick, series_bc, precision=lax.Precision.HIGHEST)
    kept_x_heads = (
        kept_x.reshape(row_reqs, edge_len, local_ssm, SSM_DIM)
        .transpose(0, 2, 1, 3)
        .reshape(row_reqs, local_ssm, edge_len * SSM_DIM)
    )
    states_out, edges_out = (
        lax.all_to_all(
            kept_states.reshape(row_reqs, local_ssm, SSM_DIM * STATE).astype(jnp.bfloat16),
            "mdl",
            split_axis=0,
            concat_axis=1,
            tiled=True,
        ).astype(jnp.float32),
        lax.all_to_all(
            kept_x_heads.astype(jnp.bfloat16), "mdl", split_axis=0, concat_axis=1, tiled=True
        ).astype(kept_x_heads.dtype),
    )
    all_ssm = states_out.shape[1]
    kept_state = states_out.reshape(own_reqs, all_ssm, SSM_DIM, STATE)
    edge_x = (
        edges_out.reshape(own_reqs, all_ssm, edge_len, SSM_DIM)
        .transpose(0, 2, 1, 3)
        .reshape(own_reqs, edge_len, all_ssm * SSM_DIM)
    )
    own_bc = lax.dynamic_slice_in_dim(kept_bc, mdl_rank * own_reqs, own_reqs, 0)
    kept_conv = jnp.concatenate([edge_x, own_bc], axis=2).astype(jnp.bfloat16)
    mixed = lax.psum_scatter(
        (
            jnp.dot(attention_flat, w_attn_out, preferred_element_type=jnp.float32)
            + jnp.dot(gated, w_mamba_out, preferred_element_type=jnp.float32)
        ).astype(jnp.bfloat16),
        "mdl",
        scatter_dimension=0,
        tiled=True,
    ).astype(jnp.float32)
    own_rows = lax.dynamic_slice_in_dim(flat_rows, mdl_rank * own_tokens, own_tokens, 0)
    after_mixer = (own_rows.astype(jnp.float32) + mixed).astype(jnp.bfloat16)
    rows_piece = lax.all_gather(after_mixer, "req", axis=0, tiled=True)
    prepared = rms_scale(rows_piece, mlp_gain).astype(jnp.bfloat16)
    gate_val = jnp.dot(prepared, w_gate, preferred_element_type=jnp.float32)
    up_val = jnp.dot(prepared, w_up, preferred_element_type=jnp.float32)
    active = (jax.nn.silu(gate_val) * up_val).astype(jnp.bfloat16)
    down_val = jnp.dot(active, w_down, preferred_element_type=jnp.float32)
    joined = jnp.concatenate([down_val, rows_piece.astype(jnp.float32)], axis=1)
    partial_value = joined[:, :width]
    column_tokens = joined.shape[0]
    summed = lax.psum(partial_value.astype(jnp.bfloat16), "req").astype(jnp.float32)
    after_feed = (joined[:, width:] + summed).astype(jnp.bfloat16)
    final_rows = rms_scale(after_feed, final_gain).astype(jnp.bfloat16)
    hidden_out = lax.dynamic_slice_in_dim(after_feed, req_rank * own_tokens, own_tokens, 0)
    vocab_here = head_weight.shape[0]
    logits = lax.dot_general(
        final_rows, head_weight, contract_last, preferred_element_type=jnp.float32
    )
    id_grid = draft_ids.reshape(req_count, mdl_count, own_reqs, draft_len)
    column_ids = lax.dynamic_index_in_dim(id_grid, mdl_rank, 1, keepdims=False)
    next_ids = jnp.concatenate([column_ids[..., 1:], column_ids[..., :1]], axis=-1).reshape(
        column_tokens
    )
    vocab_ids = req_rank * vocab_here + jnp.arange(vocab_here)
    target_part = jnp.sum(jnp.where(vocab_ids[None, :] == next_ids[:, None], logits, 0.0), axis=1)
    local_top = jnp.max(logits, axis=1)
    local_total = jnp.sum(jnp.exp(logits - local_top[:, None]), axis=1)
    top_all, total_all, target_all = joined_2(
        (local_top, local_total, target_part), "req", combine_stats
    )
    own_top = lax.dynamic_slice_in_dim(top_all, req_rank * own_tokens, own_tokens, 0)
    own_total = lax.dynamic_slice_in_dim(total_all, req_rank * own_tokens, own_tokens, 0)
    own_target = lax.dynamic_slice_in_dim(target_all, req_rank * own_tokens, own_tokens, 0)
    log_total = own_top + jnp.log(own_total)
    position = jnp.arange(own_tokens) % draft_len
    verify_scores = jnp.where(
        position < draft_len - 1, own_target - log_total, own_top - log_total
    ).reshape(own_reqs, draft_len)
    return (hidden_out.reshape(own_reqs, draft_len, width), verify_scores, kept_state, kept_conv)


def solution(mesh):
    in_specs = (
        P("req", None, None),
        P(),
        P(None, "mdl"),
        P(),
        P("mdl", None),
        P("req", None, None, None),
        P("req"),
        P("req"),
        P("req"),
        P(None, "mdl"),
        P(None, "mdl"),
        P(),
        P(None, "mdl"),
        P(None, "mdl"),
        P(),
        P("mdl"),
        P("mdl"),
        P("mdl"),
        P("req", "mdl", None, None),
        P("req", None, "mdl"),
        P("req", None, None),
        P("mdl", None),
        P(),
        P(None, "req"),
        P(None, "req"),
        P("req", None),
        P(),
        P("req", None),
        P(),
    )
    out_specs = (
        P(("req", "mdl"), None, None),
        P(("req", "mdl"), None),
        P(("req", "mdl"), None, None, None),
        P(("req", "mdl"), None, None),
    )
    return jax.shard_map(shards, mesh=mesh, in_specs=in_specs, out_specs=out_specs, check_vma=False)
```

profile of v0, /device:TPU:9, one launch (start us, length us, event | category | flops | bytes accessed | tf_op | source)
XLA Modules:
  0.0 238.5 jit_solution(2234555743490413873)
XLA Ops:
  7.9 1.3 fusion.149
  9.2 1.2 fusion.27
  10.5 1.7 fusion.150
  12.2 4.4 %compare_select_fusion.2 = s32[256,1]{0,1:T(1,128)S(1)} fusion(s32[]{:T(128)} %bitcast.7, s32[]{:T(128)} %bitcast.8, s32[]{:T(128)} %bitcast.9, s32[]{:T(128)} %bitcast.10, s32[]{:T(128)} %bitcast.11, s32[]{:T(128)} %bitcast.13, s32[]{:T(128)} %bitcast.12, s32[256,1]{0,1:T(1,128)S(1)} %bitcast.180), kind=kLoop, calls=%fused_computation.200 | loop fusion | flops 3840 | bytes 2076 | tf_op jit(solution)/shard_map/jit(_take)/gather | solution.py:113
  17.9 1.2 fusion.29
  19.2 1.2 multiply_convert_fusion
  20.8 1.3 iota_compare_fusion.6
  22.1 1.5 convolution_convert_fusion.4
  23.6 1.3 dynamic-slice_bitcast_fusion.1
  25.2 1.3 fusion.30
  26.6 1.3 fusion.32
  28.5 0.9 fusion.114
  33.7 2.0 convolution_convert_fusion.3
  36.5 0.9 fusion.107
  37.4 0.8 divide_multiply_fusion.1
  38.2 1.0 reshape.386
  39.3 1.8 fusion.46
  41.1 1.9 fusion.40
  43.1 1.1 fusion.24
  44.1 1.6 copy.127
  45.7 1.0 broadcast_multiply_fusion
  46.8 2.7 %fusion.63 = f32[8,6,64,256]{3,2,1,0:T(8,128)S(1)} fusion(f32[8,16,6,64]{3,2,1,0:T(8,128)S(1)} %broadcast_multiply_fusion, f32[8,16,512]{2,1,0:T(8,128)S(1)} %divide_multiply_fusion), kind=kOutput, calls=%fused_computation.102 | convolution fusion | flops 150994944 | bytes 3801088 | tf_op jit(solution)/shard_map/rsh,rshd,rsn->rhdn/dot_general | solution.py:230
  49.5 5.6 %fusion = (bf16[8,6,64,256]{3,0,2,1:T(8,128)(2,1)}, f32[8,6,64,256]{3,0,2,1:T(8,128)S(1)}) fusion(f32[8,6,64,256]{3,2,1,0:T(8,128)S(1)} %fusion.63, f32[8,6]{0,1:T(8,128)S(1)} %copy-done.24, f32[2,6,64,256]{3,2,1,0:T(8,128)S(1)} %copy-done.11, s32[8]{0:T(128)S(1)} %copy-done.20), kind=kOutput, calls=%fused_computation.7 | convolution fusion | flops 21233680 | bytes 8650976 | tf_op jit(solution)/shard_map/rp,phdn->rhdn/dot_general | solution.py:210
  55.8 4.4 %fusion.18 = f32[8,16,6,64]{3,1,2,0:T(8,128)S(1)} fusion(f32[8,16,6,64]{3,1,2,0:T(8,128)S(1)} %convolution_bitcast_fusion, f32[8,6,64,256]{3,0,2,1:T(8,128)S(1)} %get-tuple-element.262, f32[8,16,6,64]{3,2,1,0:T(8,128)S(1)} %reshape.386, f32[6]{0:T(128)S(1)} %copy-done.40, f32[8,16,6]{1,2,0:T(8,128)S(1)} %copy-done.16, f32[8,16,512]{2,1,0:T(8,128)S(1)} %divide_multiply_fusion), kind=kOutput, calls=%fused_computation.39 | convolution fusion | flops 151191552 | bytes 4424192 | tf_op jit(solution)/shard_map/rhdn,rtn->rthd/dot_general | solution.py:214
  60.5 2.6 %fusion.152 = f32[128,2048]{1,0:T(8,128)} fusion(bf16[128,256]{0,1:T(8,128)(2,1)} %bitcast.150, bf16[256,2048]{1,0:T(8,128)(2,1)} %param.35), kind=kOutput, calls=%fused_computation.255 | convolution fusion | flops 134217728 | bytes 2162688 | tf_op jit(solution)/shard_map/dot_general | solution.py:266
  63.1 3.9 %fusion.3 = bf16[128,2048]{1,0:T(8,128)(2,1)} fusion(f32[128,2048]{1,0:T(8,128)} %fusion.152, bf16[384,2048]{1,0:T(8,128)(2,1)} %param.52, f32[128,384]{1,0:T(8,128)S(1)} %reshape.391, bf16[128,2048]{1,0:T(8,128)(2,1)S(1)} %multiply_convert_fusion, bf16[2048,384]{1,0:T(8,128)(2,1)} %param.40), kind=kOutput, calls=%fused_computation.17 | convolution fusion | flops 403570688 | bytes 5439488 | tf_op jit(solution)/shard_map/dot_general | solution.py:267
  67.0 19.0 %reduce-scatter.2.cloned.1.call-done = bf16[32,2048]{1,0:T(8,128)(2,1)} async-done(((bf16[128,2048]{1,0:T(8,128)(2,1)}), bf16[32,2048]{1,0:T(8,128)(2,1)}) %reduce-scatter.2.cloned.1.call-update) | async-done | bytes 131088 | tf_op jit(solution)/shard_map/reduce_scatter | solution.py:264
  86.1 1.7 add_convert_fusion
  89.0 5.6 %all-to-all-start.1 = ((bf16[8,6,192]{2,1,0:T(8,128)(2,1)}), bf16[8,6,192]{2,1,0:T(8,128)(2,1)S(1)}, u32[]{:S(2)}, u32[]{:S(2)}) async-start(bf16[8,6,192]{2,1,0:T(8,128)(2,1)} %reshape.484), calls=%async_computation.2 | async-start | bytes 65536 | tf_op jit(solution)/shard_map/all_to_all | solution.py:251
  94.6 3.6 %copy.145 = bf16[8,6,16384]{2,1,0:T(8,128)(2,1)} copy(bf16[8,6,16384]{2,0,1:T(8,128)(2,1)} %bitcast.145) | data formatting | bytes 3145728 | tf_op jit(solution)/shard_map/convert_element_type | solution.py:245
  98.2 5.3 %all-to-all-start = ((bf16[8,6,16384]{2,1,0:T(8,128)(2,1)}), bf16[8,6,16384]{2,1,0:T(8,128)(2,1)}, u32[]{:S(2)}, u32[]{:S(2)}) async-start(bf16[8,6,16384]{2,1,0:T(8,128)(2,1)} %copy.145), calls=%async_computation.1 | async-start | bytes 4194304 | tf_op jit(solution)/shard_map/all_to_all | solution.py:244
  105.2 9.6 %all-gather.8.cloned.1.call-done = bf16[256,2048]{1,0:T(8,128)(2,1)} async-done(((bf16[32,2048]{1,0:T(8,128)(2,1)}), bf16[256,2048]{1,0:T(8,128)(2,1)}) %all-gather.8.cloned.1.call-update) | async-done | bytes 1048592 | tf_op jit(solution)/shard_map/all_gather | solution.py:275
  114.7 1.5 fusion.7
  116.3 2.7 %fusion.73 = f32[256,512]{1,0:T(8,128)S(1)} fusion(bf16[2048,512]{1,0:T(8,128)(2,1)} %param.54, bf16[256,2048]{1,0:T(8,128)(2,1)} %all-gather.8.cloned.1.call-done, f32[2048]{0:T(1024)S(1)} %convert_element_type.270, f32[256]{0:T(256)S(1)} %add_rsqrt_fusion.2), kind=kOutput, calls=%fused_computation.113 | convolution fusion | flops 538968064 | bytes 3679232 | tf_op jit(solution)/shard_map/dot_general | solution.py:277
  119.0 4.3 %convolution_convert_fusion = bf16[256,2048]{1,0:T(8,128)(2,1)} fusion(bf16[512,2048]{1,0:T(8,128)(2,1)S(1)} %copy-done, bf16[2048,512]{1,0:T(8,128)(2,1)} %param.55, f32[256,512]{1,0:T(8,128)S(1)} %fusion.73, bf16[256,2048]{1,0:T(8,128)(2,1)} %all-gather.8.cloned.1.call-done, f32[2048]{0:T(1024)S(1)} %convert_element_type.270, f32[256]{0:T(256)S(1)} %add_rsqrt_fusion.2), kind=kOutput, calls=%fused_computation.15 | convolution fusion | flops 1077149696 | bytes 6824960 | tf_op jit(solution)/shard_map/dot_general | solution.py:280
  123.3 21.9 %all-to-all-done = bf16[8,6,16384]{2,1,0:T(8,128)(2,1)} async-done(((bf16[8,6,16384]{2,1,0:T(8,128)(2,1)}), bf16[8,6,16384]{2,1,0:T(8,128)(2,1)}, u32[]{:S(2)}, u32[]{:S(2)}) %all-to-all-start) | async-done | bytes 1572896 | tf_op jit(solution)/shard_map/all_to_all | solution.py:244
  145.2 4.2 %copy_convert_fusion = f32[8,6,16384]{2,0,1:T(8,128)} fusion(bf16[8,6,16384]{2,1,0:T(8,128)(2,1)} %all-to-all-done), kind=kLoop, calls=%fused_computation.25 | loop fusion | flops 786432 | bytes 4718592 | tf_op jit(solution)/shard_map/convert_element_type | solution.py:250
  149.4 5.2 %reshape.411 = f32[4,2,6,16384]{3,1,0,2:T(2,128)} reshape(f32[8,6,16384]{2,0,1:T(8,128)} %copy_convert_fusion) | data formatting | bytes 6291456 | tf_op jit(solution)/shard_map/convert_element_type | solution.py:250
  154.6 5.8 %copy.162 = f32[2,4,6,16384]{3,2,1,0:T(8,128)} copy(f32[2,4,6,16384]{3,0,1,2:T(2,128)} %bitcast.144) | data formatting | bytes 6291456
  160.4 5.3 %reshape.483 = f32[2,24,64,256]{3,2,1,0:T(8,128)} reshape(f32[2,4,6,16384]{3,2,1,0:T(8,128)} %copy.162) | data formatting | bytes 6291456
  165.7 12.8 %all-reduce.2.cloned.1.call-done = bf16[256,2048]{1,0:T(8,128)(2,1)} async-done(((bf16[256,2048]{1,0:T(8,128)(2,1)}), bf16[256,2048]{1,0:T(8,128)(2,1)}) %all-reduce.2.cloned.1.call-update) | async-done | bytes 1048592 | tf_op jit(solution)/shard_map/psum | solution.py:284
  178.6 1.7 fusion.4
  180.3 19.0 %fusion.151 = (f32[256]{0:T(256)S(1)}, f32[256,4096]{1,0:T(8,128)}) fusion(bf16[4096,2048]{1,0:T(8,128)(2,1)} %param.58, bf16[256,2048]{1,0:T(8,128)(2,1)S(1)} %get-tuple-element.226, f32[2048]{0:T(1024)S(1)} %convert_element_type.277, f32[256]{0:T(256)S(1)} %add_rsqrt_fusion.1), kind=kOutput, calls=%fused_computation.254 | convolution fusion | flops 4298113024 | bytes 22030336 | tf_op jit(solution)/shard_map/dot_general | solution.py:289
  199.3 9.4 %all-gather.3 = f32[8,1,256]{2,1,0:T(1,128)S(1)} all-gather(f32[1,1,256]{2,1,0:T(1,128)S(1)} %bitcast.175), channel_id=2, replica_groups=mesh['req'=8,'mdl'=4] {'req'}, dimensions={0}, use_global_device_ids=true | all-gather | bytes 9216 | tf_op jit(solution)/shard_map/all_gather | solution.py:21
  208.7 3.6 %select_reduce_fusion = (f32[256]{0:T(256)S(1)}, f32[256]{0:T(256)S(1)}) fusion(f32[256,4096]{1,0:T(8,128)} %get-tuple-element.260, s32[4096]{0:T(1024)S(1)} %iota_add_fusion, s32[256]{0:T(256)S(1)} %eq.130, f32[256]{0:T(256)S(1)} %get-tuple-element.259), kind=kLoop, calls=%fused_computation.4 | loop fusion | flops 5242368 | bytes 4214784 | tf_op jit(solution)/shard_map/reduce_sum | solution.py:298
  212.3 8.7 %all-gather.4 = f32[8,1,256]{2,1,0:T(1,128)S(1)} all-gather(f32[1,1,256]{2,1,0:T(1,128)S(1)} %bitcast.177), channel_id=3, replica_groups=mesh['req'=8,'mdl'=4] {'req'}, dimensions={0}, use_global_device_ids=true | all-gather | bytes 9216 | tf_op jit(solution)/shard_map/all_gather | solution.py:21
  221.0 8.0 %all-gather.5 = f32[8,1,256]{2,1,0:T(1,128)S(1)} all-gather(f32[1,1,256]{2,1,0:T(1,128)S(1)} %bitcast.176), channel_id=4, replica_groups=mesh['req'=8,'mdl'=4] {'req'}, dimensions={0}, use_global_device_ids=true | all-gather | bytes 9216 | tf_op jit(solution)/shard_map/all_gather | solution.py:21
  229.1 1.6 constant_dynamic-slice_fusion.4
  (202 shorter events, 13.7 us)
Async XLA Ops:
  7.2 111.8 %copy-start = (bf16[512,2048]{1,0:T(8,128)(2,1)S(1)}, bf16[512,2048]{1,0:T(8,128)(2,1)}, u32[]{:S(2)}) copy-start(bf16[512,2048]{1,0:T(8,128)(2,1)} %param.56) | copy-start | bytes 6291460
  7.2 78.9 %reduce-scatter.2.cloned.1.call-start = ((), (), s32[]{:S(2)}) async-start(), calls=%async_computation.3 | async-start | bytes 655360 | tf_op jit(solution)/shard_map/reduce_scatter | solution.py:264
  10.5 9.9 %copy-start.10 = (bf16[2048,256]{1,0:T(8,128)(2,1)S(1)}, bf16[2048,256]{1,0:T(8,128)(2,1)}, u32[]{:S(2)}) copy-start(bf16[2048,256]{1,0:T(8,128)(2,1)} %param.33) | copy-start | bytes 3145732
  17.2 8.0 %copy-start.38 = (pred[256]{0:T(512)(128)(4,1)}, pred[256]{0:T(512)(128)(4,1)S(1)}, u32[]{:S(2)}) copy-start(pred[256]{0:T(512)(128)(4,1)S(1)} %get-tuple-element.227) | copy-start | bytes 772
  17.2 9.3 %copy-start.41 = (pred[256]{0:T(512)(128)(4,1)}, pred[256]{0:T(512)(128)(4,1)S(1)}, u32[]{:S(2)}) copy-start(pred[256]{0:T(512)(128)(4,1)S(1)} %broadcast_compare_fusion) | copy-start | bytes 772
  22.1 4.5 %copy-start.33 = (pred[1024]{0:T(1024)(128)(4,1)}, pred[1024]{0:T(1024)(128)(4,1)S(1)}, u32[]{:S(2)}) copy-start(pred[1024]{0:T(1024)(128)(4,1)S(1)} %get-tuple-element.266) | copy-start | bytes 3076
  22.1 4.5 %copy-start.31 = (pred[1024]{0:T(1024)(128)(4,1)}, pred[1024]{0:T(1024)(128)(4,1)S(1)}, u32[]{:S(2)}) copy-start(pred[1024]{0:T(1024)(128)(4,1)S(1)} %get-tuple-element.265) | copy-start | bytes 3076
  24.9 5.2 %copy-start.12 = (bf16[1024,256]{1,0:T(8,128)(2,1)}, bf16[1024,256]{1,0:T(8,128)(2,1)S(1)}, u32[]{:S(2)}) copy-start(bf16[1024,256]{1,0:T(8,128)(2,1)S(1)} %get-tuple-element.232) | copy-start | bytes 1572868
  24.9 5.2 %copy-start.14 = (bf16[1024,256]{1,0:T(8,128)(2,1)}, bf16[1024,256]{1,0:T(8,128)(2,1)S(1)}, u32[]{:S(2)}) copy-start(bf16[1024,256]{1,0:T(8,128)(2,1)S(1)} %get-tuple-element.231) | copy-start | bytes 1572868
  24.9 4.6 %copy-start.43 = (s32[8]{0:T(128)S(1)}, s32[8]{0:T(128)}, u32[]{:S(2)}) copy-start(s32[8]{0:T(128)} %param.39) | copy-start | bytes 100
  24.9 4.6 %copy-start.26 = (bf16[4,384]{1,0:T(4,128)(2,1)S(1)}, bf16[4,384]{1,0:T(4,128)(2,1)}, u32[]{:S(2)}) copy-start(bf16[4,384]{1,0:T(4,128)(2,1)} %param.44) | copy-start | bytes 9220
  24.9 4.6 %copy-start.25 = (bf16[4,512]{1,0:T(4,128)(2,1)S(1)}, bf16[4,512]{1,0:T(4,128)(2,1)}, u32[]{:S(2)}) copy-start(bf16[4,512]{1,0:T(4,128)(2,1)} %param.45) | copy-start | bytes 12292
  25.0 4.6 %copy-start.19 = (s32[8]{0:T(128)S(1)}, s32[8]{0:T(128)}, u32[]{:S(2)}) copy-start(s32[8]{0:T(128)} %param.38) | copy-start | bytes 100
  25.0 4.6 %copy-start.30 = (bf16[2,3,384]{2,0,1:T(2,128)(2,1)S(1)}, bf16[2,3,384]{2,0,1:T(2,128)(2,1)}, u32[]{:S(2)}) copy-start(bf16[2,3,384]{2,0,1:T(2,128)(2,1)} %param.50) | copy-start | bytes 13828
  25.0 4.8 %copy-start.29 = (bf16[2,3,512]{2,0,1:T(2,128)(2,1)S(1)}, bf16[2,3,512]{2,0,1:T(2,128)(2,1)}, u32[]{:S(2)}) copy-start(bf16[2,3,512]{2,0,1:T(2,128)(2,1)} %param.51) | copy-start | bytes 18436
  25.0 5.1 %copy-start.21 = (bf16[2048,6]{0,1:T(8,128)(2,1)S(1)}, bf16[2048,6]{0,1:T(8,128)(2,1)}, u32[]{:S(2)}) copy-start(bf16[2048,6]{0,1:T(8,128)(2,1)} %param.43) | copy-start | bytes 73732
  25.2 5.3 %copy-start.37 = (f32[6]{0:T(128)S(1)}, f32[6]{0:T(128)}, u32[]{:S(2)}) copy-start(f32[6]{0:T(128)} %param.47) | copy-start | bytes 76
  25.2 6.1 %copy-start.39 = (f32[6]{0:T(128)S(1)}, f32[6]{0:T(128)}, u32[]{:S(2)}) copy-start(f32[6]{0:T(128)} %param.46) | copy-start | bytes 76
  27.9 1.7 copy-start.22
  33.7 2.1 copy-start.5
  39.2 1.9 copy-start.9
  39.2 3.8 %copy-start.34 = (f32[256]{0:T(256)S(1)}, f32[256]{0:T(256)}, u32[]{:S(2)}) copy-start(f32[256]{0:T(256)} %fusion.112) | copy-start | bytes 3076
  39.3 3.8 %copy-start.13 = (bf16[1024,256]{1,0:T(8,128)(2,1)S(1)}, bf16[1024,256]{1,0:T(8,128)(2,1)}, u32[]{:S(2)}) copy-start(bf16[1024,256]{1,0:T(8,128)(2,1)} %copy-done.12) | copy-start | bytes 1572868
  39.3 3.8 %copy-start.17 = (f32[256,128]{1,0:T(8,128)S(1)}, f32[256,128]{1,0:T(8,128)}, u32[]{:S(2)}) copy-start(f32[256,128]{1,0:T(8,128)} %fusion.114) | copy-start | bytes 393220
  39.3 3.8 %copy-start.23 = (f32[256]{0:T(256)S(1)}, f32[256]{0:T(256)}, u32[]{:S(2)}) copy-start(f32[256]{0:T(256)} %copy-done.22) | copy-start | bytes 3076
  39.3 3.8 %copy-start.32 = (pred[1024]{0:T(1024)(128)(4,1)S(1)}, pred[1024]{0:T(1024)(128)(4,1)}, u32[]{:S(2)}) copy-start(pred[1024]{0:T(1024)(128)(4,1)} %copy-done.31) | copy-start | bytes 3076
  39.3 3.8 %copy-start.42 = (pred[256]{0:T(512)(128)(4,1)S(1)}, pred[256]{0:T(512)(128)(4,1)}, u32[]{:S(2)}) copy-start(pred[256]{0:T(512)(128)(4,1)} %copy-done.41) | copy-start | bytes 772
  46.8 2.7 %copy-start.11 = (f32[2,6,64,256]{3,2,1,0:T(8,128)S(1)}, f32[2,6,64,256]{3,2,1,0:T(8,128)}, u32[]{:S(2)}) copy-start(f32[2,6,64,256]{3,2,1,0:T(8,128)} %param.49) | copy-start | bytes 2359300
  46.8 2.7 %copy-start.20 = (s32[8]{0:T(128)S(1)}, s32[8]{0:T(128)}, u32[]{:S(2)}) copy-start(s32[8]{0:T(128)} %param.38) | copy-start | bytes 100
  46.8 2.7 %copy-start.24 = (f32[8,6]{0,1:T(8,128)S(1)}, f32[8,6]{0,1:T(8,128)}, u32[]{:S(2)}) copy-start(f32[8,6]{0,1:T(8,128)} %exp.83) | copy-start | bytes 580
  49.5 5.7 %copy-start.15 = (f32[8,16,16]{2,1,0:T(8,128)S(1)}, f32[8,16,16]{2,1,0:T(8,128)}, u32[]{:S(2)}) copy-start(f32[8,16,16]{2,1,0:T(8,128)} %fusion.107) | copy-start | bytes 24580
  49.5 5.7 %copy-start.18 = (f32[8,16,6]{1,2,0:T(8,128)S(1)}, f32[8,16,6]{1,2,0:T(8,128)}, u32[]{:S(2)}) copy-start(f32[8,16,6]{1,2,0:T(8,128)} %copy.133) | copy-start | bytes 9220
  49.5 5.7 %copy-start.27 = (pred[16,16]{1,0:T(8,128)(4,1)S(1)}, pred[16,16]{1,0:T(8,128)(4,1)}, u32[]{:S(2)}) copy-start(pred[16,16]{1,0:T(8,128)(4,1)} %iota_compare_fusion.5) | copy-start | bytes 772
  49.5 6.3 %copy-start.16 = (f32[8,16,6]{1,2,0:T(8,128)S(1)}, f32[8,16,6]{1,2,0:T(8,128)}, u32[]{:S(2)}) copy-start(f32[8,16,6]{1,2,0:T(8,128)} %copy.137) | copy-start | bytes 9220
  49.5 6.3 %copy-start.40 = (f32[6]{0:T(128)S(1)}, f32[6]{0:T(128)}, u32[]{:S(2)}) copy-start(f32[6]{0:T(128)} %param.48) | copy-start | bytes 76
  63.1 24.7 %copy-start.44 = (s32[8]{0:T(128)S(1)}, s32[8]{0:T(128)}, u32[]{:S(2)}) copy-start(s32[8]{0:T(128)} %param.39) | copy-start | bytes 100
  63.1 24.8 %copy-start.7 = (f32[8,16,384]{2,1,0:T(8,128)S(1)}, f32[8,16,384]{2,1,0:T(8,128)}, u32[]{:S(2)}) copy-start(f32[8,16,384]{2,1,0:T(8,128)} %copy-done.6) | copy-start | bytes 589828
  67.0 47.8 %all-gather.8.cloned.1.call-start = ((), (), s32[]{:S(2)}) async-start(), calls=%async_computation.4 | async-start | bytes 1179648 | tf_op jit(solution)/shard_map/all_gather | solution.py:275
  89.0 9.2 %all-to-all-start.1 = ((bf16[8,6,192]{2,1,0:T(8,128)(2,1)}), bf16[8,6,192]{2,1,0:T(8,128)(2,1)S(1)}, u32[]{:S(2)}, u32[]{:S(2)}) async-start(bf16[8,6,192]{2,1,0:T(8,128)(2,1)} %reshape.484), calls=%async_computation.2 | async-start | bytes 65536 | tf_op jit(solution)/shard_map/all_to_all | solution.py:251
  98.2 5.3 %copy-start.35 = (bf16[2048]{0:T(1024)(128)(2,1)S(1)}, bf16[2048]{0:T(1024)(128)(2,1)}, u32[]{:S(2)}) copy-start(bf16[2048]{0:T(1024)(128)(2,1)} %param.53) | copy-start | bytes 12292
  98.2 5.3 %copy-start.36 = (bf16[2048]{0:T(1024)(128)(2,1)S(1)}, bf16[2048]{0:T(1024)(128)(2,1)}, u32[]{:S(2)}) copy-start(bf16[2048]{0:T(1024)(128)(2,1)} %param.57) | copy-start | bytes 12292
  98.2 5.3 %copy-start.28 = (s32[64,16]{0,1:T(8,128)S(1)}, s32[64,16]{0,1:T(8,128)}, u32[]{:S(2)}) copy-start(s32[64,16]{0,1:T(8,128)} %param.59) | copy-start | bytes 12292
  98.2 5.7 %copy-start.4 = (f32[8,16,512]{2,1,0:T(8,128)S(1)}, f32[8,16,512]{2,1,0:T(8,128)}, u32[]{:S(2)}) copy-start(f32[8,16,512]{2,1,0:T(8,128)} %copy-done.3) | copy-start | bytes 786436
  98.2 47.0 %all-to-all-start = ((bf16[8,6,16384]{2,1,0:T(8,128)(2,1)}), bf16[8,6,16384]{2,1,0:T(8,128)(2,1)}, u32[]{:S(2)}, u32[]{:S(2)}) async-start(bf16[8,6,16384]{2,1,0:T(8,128)(2,1)} %copy.145), calls=%async_computation.1 | async-start | bytes 4194304 | tf_op jit(solution)/shard_map/all_to_all | solution.py:244
  103.5 75.0 %all-reduce.2.cloned.1.call-start = ((), (), s32[]{:S(2)}) async-start(), calls=%async_computation.5 | async-start | bytes 2097152 | tf_op jit(solution)/shard_map/psum | solution.py:284
  160.4 18.2 %copy-start.2 = (bf16[256,2048]{1,0:T(8,128)(2,1)S(1)}, bf16[256,2048]{1,0:T(8,128)(2,1)}, u32[]{:S(2)}) copy-start(bf16[256,2048]{1,0:T(8,128)(2,1)} %all-gather.8.cloned.1.call-done) | copy-start | bytes 3145732
  180.3 19.0 %copy-start.8 = (bf16[256,2048]{1,0:T(8,128)(2,1)}, bf16[256,2048]{1,0:T(8,128)(2,1)S(1)}, u32[]{:S(2)}) copy-start(bf16[256,2048]{1,0:T(8,128)(2,1)S(1)} %get-tuple-element.226) | copy-start | bytes 3145732
  208.7 23.2 %copy-start.1 = (bf16[512,2048]{1,0:T(8,128)(2,1)S(1)}, bf16[512,2048]{1,0:T(8,128)(2,1)}, u32[]{:S(2)}) copy-start(bf16[512,2048]{1,0:T(8,128)(2,1)} %param.56) | copy-start | bytes 6291460
  (2 other events, 2.7 us)
Sparse Core Ops, SparseCore 0:
  67.1 18.9 reduce-scatter.1
  88.5 26.1 all-gather.7
  123.4 55.0 all-reduce.1
where the time goes:
time: 241 us; the launch traced here: 238 us
  waiting for transfers between devices  63.4 us (26%)
  matrix products  58.7 us (24%)
  local copies, waits for them, and re-layouts  34.3 us (14%)
  other arithmetic  30 us (12%)
  blocking collectives  26.2 us (11%)
  between operations  14.6 us (6%)
  starting transfers between devices  11 us (5%)
    all_gather x3, blocking collectives, joined_2(): gathered = jax.tree.map(lambda a: lax.all_gather(a, axis), part)  26.2 us
    all_to_all x1, waiting for transfers between devices, shards(): lax.all_to_all(kept_states.reshape(row_reqs, local_ssm, SSM_DIM * STATE)....  21.9 us
    reduce_scatter x1, waiting for transfers between devices, shards(): lax.psum_scatter((jnp.dot(attention_flat, w_attn_out, preferred_element_t...  19 us
    dot_general x1, matrix products, shards(): lax.dot_general(final_rows, head_weight, contract_last, preferred_element...  19 us
    psum x1, waiting for transfers between devices, shards(): lax.psum(partial_value.astype(jnp.bfloat16), 'req').astype(jnp.float32)  12.8 us
    unnamed x97, local copies, waits for them, and re-layouts  11.5 us
    all_gather x1, waiting for transfers between devices, shards(): rows_piece = lax.all_gather(after_mixer, 'req', axis=0, tiled=True)  9.59 us
    dot_general x1, matrix products, shards(): jnp.einsum('rp,phdn->rhdn', prompt_pick, prompt_state, precision=lax.Prec...  5.64 us
  transfers between devices with their start and end apart: 5, of which 4 were waited for; matrix products, arithmetic and copies ran while one was open for 15% of the time, Pallas kernels for 0%

commit v1 on v0

--- a/solution.py
+++ b/solution.py
@@ -1,6 +1,10 @@
+import functools
+
 import jax
 import jax.numpy as jnp
 from jax import lax
+from jax.experimental import pallas as pl
+from jax.experimental.pallas import tpu as pltpu
 from jax.sharding import PartitionSpec as P
 
 Q_HEADS = 8
@@ -11,21 +15,12 @@
 CONV = 4
 PROMPTS = 2
 P_MAX = 1024
+DRAFT = 16
+MESH = pl.DeviceIdType.MESH
 
 
 eps_norm = 1e-05
 far_below = -1e30
-
-
-def joined_2(part, axis, combine):
-    gathered = jax.tree.map(lambda a: lax.all_gather(a, axis), part)
-
-    def take(source):
-        return jax.tree.map(lambda a: lax.dynamic_index_in_dim(a, source, 0, False), gathered)
-
-    return lax.fori_loop(
-        1, lax.axis_size(axis), lambda source, state: combine(state, take(source)), take(0)
-    )
 
 
 def rms_scale(values, gain):
@@ -42,12 +37,340 @@
     return jax.nn.silu(summed)
 
 
-def combine_stats(first, second):
-    joint_top = jnp.maximum(first[0], second[0])
-    joint_total = first[1] * jnp.exp(first[0] - joint_top) + second[1] * jnp.exp(
-        second[0] - joint_top
-    )
-    return (joint_top, joint_total, first[2] + second[2])
+def tail_kernel(
+    n,
+    m,
+    mixed_ref,
+    hidden_ref,
+    mlp_gain_ref,
+    final_gain_ref,
+    ids_ref,
+    gate_hbm,
+    up_hbm,
+    down_hbm,
+    head_hbm,
+    kept_hbm,
+    edge_hbm,
+    hidden_out_ref,
+    verify_ref,
+    kept_out,
+    edge_out,
+    gate_w,
+    up_w,
+    down_w,
+    head_w,
+    after_ref,
+    mix_in,
+    rows_ref,
+    final_ref,
+    final_t,
+    active_ref,
+    down_ref,
+    pair_in,
+    chip_send,
+    chip_in,
+    stats_ref,
+    load_sems,
+    mix_sems,
+    gather_sems,
+    final_sems,
+    pair_sems,
+    chip_sems,
+    stats_sems,
+    kept_sems,
+    edge_sems,
+):
+    req = lax.axis_index("req")
+    mdl = lax.axis_index("mdl")
+    chips = n // 2
+    chip = req // 2
+    core = req % 2
+    sibling = chip * 2 + (1 - core)
+    block = after_ref.shape[0]
+    width = after_ref.shape[1]
+    tokens = n * block
+    own_reqs = kept_out.shape[0]
+    heads = kept_hbm.shape[1]
+
+    loads = [
+        pltpu.make_async_copy(src, dst, load_sems.at[i])
+        for i, (src, dst) in enumerate(
+            ((gate_hbm, gate_w), (up_hbm, up_w), (down_hbm, down_w), (head_hbm, head_w))
+        )
+    ]
+    for load in loads:
+        load.start()
+
+    barrier = pltpu.get_barrier_semaphore()
+    for d in range(1, m):
+        pl.semaphore_signal(
+            barrier, inc=1, device_id=(req, (mdl + d) % m), device_id_type=MESH
+        )
+    for d in range(1, n):
+        pl.semaphore_signal(
+            barrier, inc=1, device_id=((req + d) % n, mdl), device_id_type=MESH
+        )
+    pl.semaphore_wait(barrier, m - 1 + n - 1)
+
+    def send(src, dst, sems, index, device):
+        copy = pltpu.make_async_remote_copy(
+            src_ref=src,
+            dst_ref=dst,
+            send_sem=sems.at[0, index],
+            recv_sem=sems.at[1, index],
+            device_id=device,
+            device_id_type=MESH,
+        )
+        copy.start()
+        return copy
+
+    mixes = []
+    for d in range(1, m):
+        to = (mdl + d) % m
+        mixes.append(
+            send(
+                mixed_ref.at[pl.ds(to * block, block)],
+                mix_in.at[d - 1],
+                mix_sems,
+                d - 1,
+                (req, to),
+            )
+        )
+    total = mixed_ref[pl.ds(mdl * block, block)].astype(jnp.float32)
+    for copy in mixes:
+        copy.wait_recv()
+    for d in range(m - 1):
+        total = total + mix_in[d].astype(jnp.float32)
+    after = (
+        hidden_ref[pl.ds(mdl * block, block)].astype(jnp.float32) + total
+    ).astype(jnp.bfloat16)
+    after_ref[...] = after
+    rows_ref[req] = rms_scale(after, mlp_gain_ref[...]).astype(jnp.bfloat16)
+
+    def gather_rows(buffer, sems):
+        sent = [send(buffer.at[req], buffer.at[req], sems, 0, (sibling, mdl))]
+        across = []
+        for c in range(1, chips):
+            to = (chip + c) % chips * 2 + core
+            across.append(send(buffer.at[req], buffer.at[req], sems, c, (to, mdl)))
+        for c in range(1, chips):
+            across[c - 1].wait_recv()
+            source = (chip + chips - c) % chips * 2 + core
+            sent.append(
+                send(buffer.at[source], buffer.at[source], sems, chips - 1 + c, (sibling, mdl))
+            )
+        for copy in sent:
+            copy.wait_recv()
+        return sent + across
+
+    waits = gather_rows(rows_ref, gather_sems)
+
+    moves = []
+    for d in range(1, m):
+        to = (mdl + d) % m
+        moves.append(
+            send(
+                kept_hbm.at[pl.ds(to * own_reqs, own_reqs)],
+                kept_out.at[:, pl.ds(mdl * heads, heads)],
+                kept_sems,
+                d - 1,
+                (req, to),
+            )
+        )
+        moves.append(
+            send(
+                edge_hbm.at[pl.ds(to * own_reqs, own_reqs)],
+                edge_out.at[mdl],
+                edge_sems,
+                d - 1,
+                (req, to),
+            )
+        )
+    own_kept = pltpu.make_async_copy(
+        kept_hbm.at[pl.ds(mdl * own_reqs, own_reqs)],
+        kept_out.at[:, pl.ds(mdl * heads, heads)],
+        load_sems.at[4],
+    )
+    own_edge = pltpu.make_async_copy(
+        edge_hbm.at[pl.ds(mdl * own_reqs, own_reqs)], edge_out.at[mdl], load_sems.at[5]
+    )
+    own_kept.start()
+    own_edge.start()
+
+    for load in loads[:3]:
+        load.wait()
+    units = gate_w.shape[1]
+    unit_step = min(units, 256)
+    group = 256 // block
+    column_step = 512
+
+    @pl.loop(0, n // group)
+    def _(part):
+        first = part * group
+        prepared = rows_ref[pl.ds(first, group)].reshape(256, width)
+
+        @pl.loop(0, units // unit_step)
+        def _(step):
+            at = pl.ds(pl.multiple_of(step * unit_step, unit_step), unit_step)
+            gate_val = jnp.dot(prepared, gate_w[:, at], preferred_element_type=jnp.float32)
+            up_val = jnp.dot(prepared, up_w[:, at], preferred_element_type=jnp.float32)
+            active_ref[:, at] = (jax.nn.silu(gate_val) * up_val).astype(jnp.bfloat16)
+
+        @pl.loop(0, width // column_step)
+        def _(step):
+            at = pl.ds(pl.multiple_of(step * column_step, column_step), column_step)
+            value = jnp.dot(active_ref[...], down_w[:, at], preferred_element_type=jnp.float32)
+            down_ref[pl.ds(first, group), :, at] = value.astype(jnp.bfloat16).reshape(
+                group, block, column_step
+            )
+
+    pairs = []
+    for c in range(chips):
+        to_chip = (chip + 1 + c) % chips
+        pairs.append(
+            send(
+                down_ref.at[to_chip * 2 + (1 - core)],
+                pair_in.at[c],
+                pair_sems,
+                c,
+                (sibling, mdl),
+            )
+        )
+    for c in range(chips - 1):
+        to = (chip + 1 + c) % chips * 2 + core
+        pairs[c].wait_recv()
+        chip_send[c] = (
+            down_ref[to].astype(jnp.float32) + pair_in[c].astype(jnp.float32)
+        ).astype(jnp.bfloat16)
+        waits.append(send(chip_send.at[c], chip_in.at[c], chip_sems, c, (to, mdl)))
+    pairs[chips - 1].wait_recv()
+    summed = down_ref[req].astype(jnp.float32) + pair_in[chips - 1].astype(jnp.float32)
+    for c in range(chips - 1):
+        waits[-(chips - 1) + c].wait_recv()
+        summed = summed + chip_in[c].astype(jnp.float32)
+    result = (after_ref[...].astype(jnp.float32) + summed).astype(jnp.bfloat16)
+    hidden_out_ref[...] = result
+    final_ref[req] = rms_scale(result, final_gain_ref[...]).astype(jnp.bfloat16)
+    waits += pairs
+    waits += gather_rows(final_ref, final_sems)
+
+    @pl.loop(0, width // 256)
+    def _(step):
+        at = pl.ds(pl.multiple_of(step * 256, 256), 256)
+        final_t[at, :] = (
+            final_ref[:, :, at].reshape(tokens, 256).astype(jnp.float32).T.astype(jnp.bfloat16)
+        )
+
+    loads[3].wait()
+    vocab_here = head_w.shape[0]
+    vocab_step = 512
+    ids = ids_ref[0:1, :]
+    start = (
+        jnp.full((1, tokens), far_below, jnp.float32),
+        jnp.zeros((1, tokens), jnp.float32),
+        jnp.zeros((1, tokens), jnp.float32),
+    )
+
+    def head_step(step, carry):
+        top, weight, target = carry
+        first = pl.multiple_of(step * vocab_step, vocab_step)
+        logits = jnp.dot(
+            head_w[pl.ds(first, vocab_step), :], final_t[...], preferred_element_type=jnp.float32
+        )
+        vocab_ids = (
+            req * vocab_here + first + lax.broadcasted_iota(jnp.int32, (vocab_step, tokens), 0)
+        )
+        target = target + jnp.sum(
+            jnp.where(vocab_ids == ids, logits, 0.0), axis=0, keepdims=True
+        )
+        new_top = jnp.maximum(top, jnp.max(logits, axis=0, keepdims=True))
+        weight = weight * jnp.exp(top - new_top) + jnp.sum(
+            jnp.exp(logits - new_top), axis=0, keepdims=True
+        )
+        return (new_top, weight, target)
+
+    top, weight, target = lax.fori_loop(0, vocab_here // vocab_step, head_step, start)
+    stats_ref[req] = jnp.concatenate(
+        [top, weight, target, jnp.zeros((5, tokens), jnp.float32)], axis=0
+    )
+    shares = [
+        send(stats_ref.at[req], stats_ref.at[req], stats_sems, d - 1, ((req + d) % n, mdl))
+        for d in range(1, n)
+    ]
+    for copy in shares:
+        copy.wait_recv()
+    stats = stats_ref[...]
+    tops, weights, targets = stats[:, 0:1, :], stats[:, 1:2, :], stats[:, 2:3, :]
+    top = jnp.max(tops, axis=0)
+    log_total = top + jnp.log(jnp.sum(weights * jnp.exp(tops - top[None]), axis=0))
+    target = jnp.sum(targets, axis=0)
+    position = lax.broadcasted_iota(jnp.int32, (1, tokens), 1) % DRAFT
+    score = jnp.where(position < DRAFT - 1, target, top) - log_total
+    verify_ref[...] = jnp.broadcast_to(score, verify_ref.shape)
+
+    for copy in mixes + waits + shares:
+        copy.wait_send()
+    for copy in moves:
+        copy.wait()
+    own_kept.wait()
+    own_edge.wait()
+
+
+def run_tail(
+    mixed, hidden, mlp_gain, final_gain, ids, w_gate, w_up, w_down, head_weight, kept, edges
+):
+    n = lax.axis_size("req")
+    m = lax.axis_size("mdl")
+    chips = n // 2
+    row_tokens, width = hidden.shape
+    block = row_tokens // m
+    tokens = n * block
+    row_reqs, heads = kept.shape[:2]
+    own_reqs = row_reqs // m
+    vmem = pl.BlockSpec(memory_space=pltpu.VMEM)
+    anywhere = pl.BlockSpec(memory_space=pl.ANY)
+    bf16 = jnp.bfloat16
+    sems = pltpu.SemaphoreType.DMA
+    return pl.pallas_call(
+        functools.partial(tail_kernel, n, m),
+        out_shape=(
+            jax.ShapeDtypeStruct((block, width), bf16),
+            jax.ShapeDtypeStruct((8, tokens), jnp.float32),
+            jax.ShapeDtypeStruct((own_reqs, heads * m) + kept.shape[2:], bf16),
+            jax.ShapeDtypeStruct((m, own_reqs) + edges.shape[1:], bf16),
+        ),
+        in_specs=[vmem] * 5 + [anywhere] * 6,
+        out_specs=(vmem, vmem, anywhere, anywhere),
+        scratch_shapes=[
+            pltpu.VMEM(w_gate.shape, bf16),
+            pltpu.VMEM(w_up.shape, bf16),
+            pltpu.VMEM(w_down.shape, bf16),
+            pltpu.VMEM(head_weight.shape, bf16),
+            pltpu.VMEM((block, width), bf16),
+            pltpu.VMEM((m - 1, block, width), bf16),
+            pltpu.VMEM((n, block, width), bf16),
+            pltpu.VMEM((n, block, width), bf16),
+            pltpu.VMEM((width, tokens), bf16),
+            pltpu.VMEM((256, w_gate.shape[1]), bf16),
+            pltpu.VMEM((n, block, width), bf16),
+            pltpu.VMEM((chips, block, width), bf16),
+            pltpu.VMEM((chips - 1, block, width), bf16),
+            pltpu.VMEM((chips - 1, block, width), bf16),
+            pltpu.VMEM((n, 8, tokens), jnp.float32),
+            sems((6,)),
+            sems((2, m - 1)),
+            sems((2, 2 * chips - 1)),
+            sems((2, 2 * chips - 1)),
+            sems((2, chips)),
+            sems((2, chips - 1)),
+            sems((2, n - 1)),
+            sems((2, m - 1)),
+            sems((2, m - 1)),
+        ],
+        compiler_params=pltpu.CompilerParams(
+            collective_id=0, has_side_effects=True, vmem_limit_bytes=50 * 1024 * 1024
+        ),
+    )(mixed, hidden, mlp_gain, final_gain, ids, w_gate, w_up, w_down, head_weight, kept, edges)
 
 
 def shards(
@@ -235,79 +558,37 @@
     )
     kept_x = jnp.einsum("rkl,rlc->rkc", window_pick, series_x, precision=lax.Precision.HIGHEST)
     kept_bc = jnp.einsum("rkl,rlc->rkc", window_pick, series_bc, precision=lax.Precision.HIGHEST)
-    kept_x_heads = (
-        kept_x.reshape(row_reqs, edge_len, local_ssm, SSM_DIM)
-        .transpose(0, 2, 1, 3)
-        .reshape(row_reqs, local_ssm, edge_len * SSM_DIM)
-    )
-    states_out, edges_out = (
-        lax.all_to_all(
-            kept_states.reshape(row_reqs, local_ssm, SSM_DIM * STATE).astype(jnp.bfloat16),
-            "mdl",
-            split_axis=0,
-            concat_axis=1,
-            tiled=True,
-        ).astype(jnp.float32),
-        lax.all_to_all(
-            kept_x_heads.astype(jnp.bfloat16), "mdl", split_axis=0, concat_axis=1, tiled=True
-        ).astype(kept_x_heads.dtype),
-    )
-    all_ssm = states_out.shape[1]
-    kept_state = states_out.reshape(own_reqs, all_ssm, SSM_DIM, STATE)
-    edge_x = (
-        edges_out.reshape(own_reqs, all_ssm, edge_len, SSM_DIM)
-        .transpose(0, 2, 1, 3)
-        .reshape(own_reqs, edge_len, all_ssm * SSM_DIM)
-    )
-    own_bc = lax.dynamic_slice_in_dim(kept_bc, mdl_rank * own_reqs, own_reqs, 0)
-    kept_conv = jnp.concatenate([edge_x, own_bc], axis=2).astype(jnp.bfloat16)
-    mixed = lax.psum_scatter(
-        (
-            jnp.dot(attention_flat, w_attn_out, preferred_element_type=jnp.float32)
-            + jnp.dot(gated, w_mamba_out, preferred_element_type=jnp.float32)
-        ).astype(jnp.bfloat16),
-        "mdl",
-        scatter_dimension=0,
-        tiled=True,
-    ).astype(jnp.float32)
-    own_rows = lax.dynamic_slice_in_dim(flat_rows, mdl_rank * own_tokens, own_tokens, 0)
-    after_mixer = (own_rows.astype(jnp.float32) + mixed).astype(jnp.bfloat16)
-    rows_piece = lax.all_gather(after_mixer, "req", axis=0, tiled=True)
-    prepared = rms_scale(rows_piece, mlp_gain).astype(jnp.bfloat16)
-    gate_val = jnp.dot(prepared, w_gate, preferred_element_type=jnp.float32)
-    up_val = jnp.dot(prepared, w_up, preferred_element_type=jnp.float32)
-    active = (jax.nn.silu(gate_val) * up_val).astype(jnp.bfloat16)
-    down_val = jnp.dot(active, w_down, preferred_element_type=jnp.float32)
-    joined = jnp.concatenate([down_val, rows_piece.astype(jnp.float32)], axis=1)
-    partial_value = joined[:, :width]
-    column_tokens = joined.shape[0]
-    summed = lax.psum(partial_value.astype(jnp.bfloat16), "req").astype(jnp.float32)
-    after_feed = (joined[:, width:] + summed).astype(jnp.bfloat16)
-    final_rows = rms_scale(after_feed, final_gain).astype(jnp.bfloat16)
-    hidden_out = lax.dynamic_slice_in_dim(after_feed, req_rank * own_tokens, own_tokens, 0)
-    vocab_here = head_weight.shape[0]
-    logits = lax.dot_general(
-        final_rows, head_weight, contract_last, preferred_element_type=jnp.float32
-    )
+    edges = jnp.pad(kept_x.astype(jnp.bfloat16), ((0, 0), (0, 16 - edge_len), (0, 0)))
+    mixed = (
+        jnp.dot(attention_flat, w_attn_out, preferred_element_type=jnp.float32)
+        + jnp.dot(gated, w_mamba_out, preferred_element_type=jnp.float32)
+    ).astype(jnp.bfloat16)
     id_grid = draft_ids.reshape(req_count, mdl_count, own_reqs, draft_len)
     column_ids = lax.dynamic_index_in_dim(id_grid, mdl_rank, 1, keepdims=False)
-    next_ids = jnp.concatenate([column_ids[..., 1:], column_ids[..., :1]], axis=-1).reshape(
-        column_tokens
-    )
-    vocab_ids = req_rank * vocab_here + jnp.arange(vocab_here)
-    target_part = jnp.sum(jnp.where(vocab_ids[None, :] == next_ids[:, None], logits, 0.0), axis=1)
-    local_top = jnp.max(logits, axis=1)
-    local_total = jnp.sum(jnp.exp(logits - local_top[:, None]), axis=1)
-    top_all, total_all, target_all = joined_2(
-        (local_top, local_total, target_part), "req", combine_stats
-    )
-    own_top = lax.dynamic_slice_in_dim(top_all, req_rank * own_tokens, own_tokens, 0)
-    own_total = lax.dynamic_slice_in_dim(total_all, req_rank * own_tokens, own_tokens, 0)
-    own_target = lax.dynamic_slice_in_dim(target_all, req_rank * own_tokens, own_tokens, 0)
-    log_total = own_top + jnp.log(own_total)
-    position = jnp.arange(own_tokens) % draft_len
-    verify_scores = jnp.where(
-        position < draft_len - 1, own_target - log_total, own_top - log_total
+    next_ids = jnp.concatenate([column_ids[..., 1:], column_ids[..., :1]], axis=-1).reshape(1, -1)
+    hidden_out, scores_all, kept_all, edges_all = run_tail(
+        mixed,
+        flat_rows,
+        mlp_gain.reshape(1, width),
+        final_gain.reshape(1, width),
+        jnp.broadcast_to(next_ids, (8, next_ids.shape[1])),
+        w_gate,
+        w_up,
+        w_down,
+        head_weight,
+        kept_states.astype(jnp.bfloat16),
+        edges,
+    )
+    kept_state = kept_all.astype(jnp.float32)
+    edge_x = (
+        edges_all[:, :, :edge_len]
+        .transpose(1, 2, 0, 3)
+        .reshape(own_reqs, edge_len, mdl_count * local_inner)
+    )
+    own_bc = lax.dynamic_slice_in_dim(kept_bc, mdl_rank * own_reqs, own_reqs, 0)
+    kept_conv = jnp.concatenate([edge_x, own_bc.astype(jnp.bfloat16)], axis=2)
+    verify_scores = lax.dynamic_slice_in_dim(
+        scores_all[0], req_rank * own_tokens, own_tokens, 0
     ).reshape(own_reqs, draft_len)
     return (hidden_out.reshape(own_reqs, draft_len, width), verify_scores, kept_state, kept_conv)
 

time: 241 us -> 121 us (0.50)
  waiting for transfers between devices: 63.4 us -> 0 us
  Pallas kernels: 0 us -> 62.2 us
  matrix products: 58.7 us -> 31.3 us
  blocking collectives: 26.2 us -> 0 us
  local copies, waits for them, and re-layouts: 34.3 us -> 10.5 us
  other arithmetic: 30 us -> 13.9 us
  between operations: 14.6 us -> 1.41 us
  starting transfers between devices: 11 us -> 0 us
    pallas_call x0 -> x1, Pallas kernels: none -> 62.2 us  [run_tail(): pl.pallas_call(functools.partial(tail_kernel, n, m), out_shape=(jax.Shape...]
    all_gather x3 -> x0, blocking collectives: 26.2 us -> none  [joined_2(): gathered = jax.tree.map(lambda a: lax.all_gather(a, axis), part)]
    dot_general x3 -> x1, matrix products: 26 us -> 0.16 us  [shards(): jnp.einsum('rt,rth->rh', pick_step, log_decay, precision=lax.Precision.HI...]
    all_to_all x2 -> x0, waiting for transfers between devices: 21.9 us -> none  [the longest x1 21.9 us: shards(): lax.all_to_all(kept_states.reshape(row_reqs, local_ssm, SSM_DIM * STATE)....]
    reduce_scatter x1 -> x0, waiting for transfers between devices: 19 us -> none  [shards(): lax.psum_scatter((jnp.dot(attention_flat, w_attn_out, preferred_element_t...]
    psum x1 -> x0, waiting for transfers between devices: 12.8 us -> none  [shards(): lax.psum(partial_value.astype(jnp.bfloat16), 'req').astype(jnp.float32)]
    all_to_all x2 -> x0, starting transfers between devices: 10.9 us -> none  [the longest x1 5.62 us: shards(): lax.all_to_all(kept_x_heads.astype(jnp.bfloat16), 'mdl', split_axis=0, co...]
    convert_element_type x8 -> x0, local copies, waits for them, and re-layouts: 9.78 us -> none  [the longest x3 5.33 us: shards(): states_out, edges_out = (lax.all_to_all(kept_states.reshape(row_reqs, loc...]
  transfers between devices with their start and end apart: 5 -> 0, of which waited for: 4 -> 0; matrix products, arithmetic and copies ran while one was open for 15% -> 0% of each run, Pallas kernels for 0% -> 0%
where the time goes in v1:
time: 121 us; the launch traced here: 119 us
  Pallas kernels  62.2 us (51%)
  matrix products  31.3 us (26%)
  other arithmetic  13.9 us (11%)
  local copies, waits for them, and re-layouts  10.5 us (9%)
  between operations  1.41 us (1%)
    pallas_call x1, Pallas kernels, run_tail(): pl.pallas_call(functools.partial(tail_kernel, n, m), out_shape=(jax.Shape...  62.2 us
    dot_general x1, matrix products, shards(): jnp.einsum('rsh,rshd,rsn->rhdn', carry_weights, heads_x, b_part, precisio...  6.53 us
    dot_general x1, matrix products, shards(): jnp.einsum('rhdn,rtn->rthd', initial, c_part, precision=lax.Precision.HIG...  4.57 us
    gather x2, other arithmetic, shards(): row_member = jnp.take(member, row_request)  4.36 us
    dot_general x1, matrix products, shards(): jnp.einsum('rp,phdn->rhdn', prompt_pick, prompt_state, precision=lax.Prec...  3.48 us
    dot_general x1, matrix products, shards(): jnp.dot(gated, w_mamba_out, preferred_element_type=jnp.float32)  3.28 us
    dot_general x1, matrix products, shards(): jnp.dot(attention_flat, w_attn_out, preferred_element_type=jnp.float32)  2.65 us

profile of v1, /device:TPU:9, one launch (start us, length us, event | category | flops | bytes accessed | tf_op | source)
XLA Modules:
  0.0 119.3 jit_solution(15346152978498030965)
XLA Ops:
  0.7 2.4 %dynamic-slice_bitcast_fusion.1 = (bf16[1024,256]{1,0:T(8,128)(2,1)}, bf16[1024,256]{1,0:T(8,128)(2,1)}) fusion(bf16[2,2,1024,256]{3,2,1,0:T(8,128)(2,1)} %param.34, s32[]{:T(128)S(6)} %select_n.122, s32[]{:T(128)S(6)} %add.218), kind=kLoop, calls=%fused_computation.58 | loop fusion | bytes 2097160 | tf_op jit(solution)/shard_map/squeeze | solution.py:449
  3.1 0.7 fusion.125
  3.8 4.3 %compare_select_fusion.2 = s32[256,1]{0,1:T(1,128)S(1)} fusion(s32[]{:T(128)} %bitcast.3, s32[]{:T(128)} %bitcast.4, s32[]{:T(128)} %bitcast.5, s32[]{:T(128)} %bitcast.6, s32[]{:T(128)} %bitcast.7, s32[]{:T(128)} %bitcast.9, s32[]{:T(128)} %bitcast.8, s32[256,1]{0,1:T(1,128)S(1)} %bitcast.125), kind=kLoop, calls=%fused_computation.160 | loop fusion | flops 3840 | bytes 2076 | tf_op jit(solution)/shard_map/jit(_take)/gather | solution.py:436
  8.1 0.7 broadcast_compare_fusion.1
  8.8 0.2 fusion.18
  9.1 0.2 multiply_convert_fusion
  9.3 1.8 %fusion.16 = bf16[16,2,8,128]{3,2,1,0:T(8,128)(2,1)S(1)} fusion(bf16[128,2048]{1,0:T(8,128)(2,1)S(1)} %multiply_convert_fusion, bf16[2048,256]{1,0:T(8,128)(2,1)} %param.31), kind=kOutput, calls=%fused_computation.28 | convolution fusion | flops 134250496 | bytes 1638400 | tf_op jit(solution)/shard_map/dot_general | solution.py:425
  11.2 0.6 fusion.124
  11.8 1.3 %iota_compare_fusion.6 = (pred[1024]{0:T(1024)(128)(4,1)S(1)}, pred[1024]{0:T(1024)(128)(4,1)S(1)}) fusion(s32[]{:T(128)} %bitcast.20, s32[]{:T(128)} %bitcast.11), kind=kLoop, calls=%fused_computation.156 | loop fusion | flops 2048 | bytes 2056 | tf_op jit(solution)/shard_map/lt | solution.py:461
  13.1 0.4 fusion.23
  13.5 0.4 fusion.21
  13.9 0.2 fusion.20
  14.2 0.3 convolution_convert_fusion.3
  14.5 0.2 select_reduce_fusion
  14.7 0.6 fusion.27
  15.5 0.4 fusion.33
  15.9 0.3 fusion.90
  16.2 0.4 fusion.15
  16.8 2.6 %fusion.126 = f32[128,2048]{1,0:T(8,128)} fusion(bf16[128,256]{0,1:T(8,128)(2,1)S(1)} %bitcast.111, bf16[256,2048]{1,0:T(8,128)(2,1)} %param.33), kind=kOutput, calls=%fused_computation.210 | convolution fusion | flops 134217728 | bytes 2162688 | tf_op jit(solution)/shard_map/dot_general | solution.py:563
  19.5 0.5 convolution_convert_fusion.2
  20.0 0.2 fusion.110
  20.2 0.4 copy-done.7
  20.6 0.6 copy-done.17
  21.3 0.2 divide_multiply_fusion.1
  21.4 0.9 reshape.353
  22.4 0.4 convolution_convert_fusion
  22.9 0.2 fusion.108
  23.1 0.4 copy-done.5
  23.6 0.2 divide_multiply_fusion
  23.8 0.9 fusion.83
  24.6 0.2 fusion.17
  25.5 2.4 %convolution_bitcast_fusion = f32[8,16,6,64]{3,1,2,0:T(8,128)} fusion(f32[8,16,6,64]{3,2,1,0:T(8,128)} %reshape.353, f32[8,16,6]{1,2,0:T(8,128)S(1)} %copy.72, f32[8,16,16]{2,1,0:T(8,128)} %fusion.83, f32[8,16,6]{1,2,0:T(8,128)S(1)} %copy.69, pred[16,16]{1,0:T(8,128)(4,1)S(1)} %iota_compare_fusion.5), kind=kOutput, calls=%fused_computation.14 | convolution fusion | flops 9486336 | bytes 407808 | tf_op jit(solution)/shard_map/rtsh,rshp->rthp/dot_general | solution.py:532
  28.0 0.2 fusion.127
  28.2 1.7 %exponential_multiply_fusion = (f32[8,16,6]{2,0,1:T(8,128)}, f32[8,16,6]{2,0,1:T(8,128)S(1)}) fusion(f32[8,16,6]{2,0,1:T(8,128)} %copy-done.13, f32[8,6]{1,0:T(8,128)S(1)} %bitcast.118, pred[8,16]{0,1:T(8,128)(4,1)S(1)} %get-tuple-element.28, f32[8,16,6]{2,0,1:T(8,128)} %copy-done.12, f32[6]{0:T(128)S(1)} %copy-done.31), kind=kLoop, calls=%fused_computation.129 | loop fusion | flops 7680 | bytes 12632 | tf_op jit(solution)/shard_map/mul | solution.py:549
  29.9 0.7 copy.76
  30.6 3.5 %fusion.31 = f32[8,6,64,256]{3,0,2,1:T(8,128)S(1)} fusion(f32[2,6,64,256]{3,2,1,0:T(8,128)} %param.47, s32[8]{0:T(128)S(1)} %copy-done.21), kind=kOutput, calls=%fused_computation.50 | convolution fusion | flops 18874384 | bytes 3932192 | tf_op jit(solution)/shard_map/rp,phdn->rhdn/dot_general | solution.py:533
  34.2 4.6 %fusion.9 = f32[8,16,6,64]{3,1,2,0:T(8,128)S(1)} fusion(f32[8,16,6,64]{3,1,2,0:T(8,128)S(1)} %copy-done.8, f32[8,6,64,256]{3,0,2,1:T(8,128)S(1)} %fusion.31, f32[8,16,6,64]{3,2,1,0:T(8,128)S(1)} %copy-done.4, f32[6]{0:T(128)S(1)} %copy-done.34, f32[8,16,6]{1,2,0:T(8,128)S(1)} %copy-done.20, f32[8,16,512]{2,1,0:T(8,128)S(1)} %divide_multiply_fusion), kind=kOutput, calls=%fused_computation.16 | convolution fusion | flops 151191552 | bytes 4424192 | tf_op jit(solution)/shard_map/rhdn,rtn->rthd/dot_general | solution.py:537
  38.9 0.8 reshape.358
  39.7 3.3 %fusion.2.mixed_ref = bf16[128,2048]{1,0:T(8,128)(2,1)S(1)} fusion(f32[128,2048]{1,0:T(8,128)} %fusion.126, bf16[384,2048]{1,0:T(8,128)(2,1)} %param.50, f32[128,384]{1,0:T(8,128)} %reshape.358, bf16[128,2048]{1,0:T(8,128)(2,1)} %copy-done.3, bf16[2048,384]{1,0:T(8,128)(2,1)} %param.38), kind=kOutput, calls=%fused_computation.4 | convolution fusion | flops 403570688 | bytes 5439488 | tf_op jit(solution)/shard_map/dot_general | solution.py:564
  43.0 1.2 %broadcast_multiply_fusion = f32[8,16,6,64]{3,2,1,0:T(8,128)S(1)} fusion(f32[8,16,6,64]{3,2,1,0:T(8,128)} %reshape.353, f32[8,16,6]{2,1,0:T(8,128)S(1)} %copy.81), kind=kLoop, calls=%fused_computation.94 | loop fusion | flops 49152 | bytes 396288 | tf_op jit(solution)/shard_map/rsh,rshd,rsn->rhdn/dot_general | solution.py:553
  44.4 6.5 %add_convert_fusion.kept_hbm = bf16[8,6,64,256]{3,2,1,0:T(8,128)(2,1)} fusion(f32[8,6,64,256]{3,0,2,1:T(8,128)} %copy-done.2, f32[8,6]{1,0:T(8,128)S(1)} %exp.54, f32[8,16,6,64]{3,2,1,0:T(8,128)S(1)} %broadcast_multiply_fusion, f32[8,16,512]{2,1,0:T(8,128)S(1)} %divide_multiply_fusion), kind=kOutput, calls=%fused_computation | convolution fusion | flops 153354240 | bytes 5378048 | tf_op jit(solution)/shard_map/rsh,rshd,rsn->rhdn/dot_general | solution.py:553
  51.3 1.2 %convolution_convert_fusion.5 = bf16[8,3,384]{2,1,0:T(4,128)(2,1)S(1)} fusion(f32[8,3,384]{2,1,0:T(4,128)S(1)} %copy-done.18, f32[8,16,384]{2,1,0:T(8,128)} %copy-done.7, s32[8,3]{1,0:T(8,128)S(1)} %iota_add_fusion), kind=kOutput, calls=%fused_computation.29 | convolution fusion | flops 2169288 | bytes 252000 | tf_op jit(solution)/shard_map/rkl,rlc->rkc/dot_general | solution.py:559
  52.6 62.2 %shard_map.300 = (bf16[32,2048]{1,0:T(8,128)(2,1)S(1)}, f32[8,256]{1,0:T(8,128)S(1)}, bf16[2,24,64,256]{3,2,1,0:T(8,128)(2,1)S(1)}, bf16[4,2,16,384]{3,2,1,0:T(8,128)(2,1)S(1)}) custom-call(bf16[128,2048]{1,0:T(8,128)(2,1)S(1)} %fusion.2.mixed_ref, bf16[128,2048]{1,0:T(8,128)(2,1)S(1)} %bitcast.106, bf16[1,2048]{1,0:T(2,128)(2,1)S(1)} %reshape.359.mlp_gain_ref, ...), custom_call_target="tpu_custom_call" | custom-call | tf_op jit(solution)/shard_map/pallas_call | solution.py:334
  114.8 2.1 %convert_element_type.199 = f32[2,24,64,256]{3,2,1,0:T(8,128)} convert(bf16[2,24,64,256]{3,2,1,0:T(8,128)(2,1)S(1)} %get-tuple-element.10) | non-fusion elementwise | flops 786432 | bytes 4718592 | tf_op jit(solution)/shard_map/convert_element_type | solution.py:582
  117.0 0.3 fusion.44
  117.3 0.6 pad_maximum_fusion.4
  118.0 0.6 reshape.363
  118.7 0.7 copy.113
  (121 shorter events, 2.1 us)
Async XLA Ops:
  0.6 21.7 %copy-start = (bf16[2048,512]{1,0:T(8,128)(2,1)S(1)}, bf16[2048,512]{1,0:T(8,128)(2,1)}, u32[]{:S(2)}) copy-start(bf16[2048,512]{1,0:T(8,128)(2,1)} %param.40) | copy-start | bytes 6291460
  0.6 2.4 %copy-start.21 = (s32[8]{0:T(128)S(1)}, s32[8]{0:T(128)}, u32[]{:S(2)}) copy-start(s32[8]{0:T(128)} %param.36) | copy-start | bytes 100
  0.7 8.1 %copy-start.1 = (bf16[8,16,2048]{2,1,0:T(8,128)(2,1)S(1)}, bf16[8,16,2048]{2,1,0:T(8,128)(2,1)}, u32[]{:S(2)}) copy-start(bf16[8,16,2048]{2,1,0:T(8,128)(2,1)} %param.29) | copy-start | bytes 1572868
  0.7 8.4 %copy-start.28 = (bf16[2048]{0:T(1024)(128)(2,1)S(1)}, bf16[2048]{0:T(1024)(128)(2,1)}, u32[]{:S(2)}) copy-start(bf16[2048]{0:T(1024)(128)(2,1)} %param.30) | copy-start | bytes 12292
  3.1 8.1 %copy-start.32 = (s32[2]{0:T(128)S(1)}, s32[2]{0:T(128)}, u32[]{:S(2)}) copy-start(s32[2]{0:T(128)} %param.35) | copy-start | bytes 28
  9.1 4.0 %copy-start.15 = (bf16[1024,256]{1,0:T(8,128)(2,1)S(1)}, bf16[1024,256]{1,0:T(8,128)(2,1)}, u32[]{:S(2)}) copy-start(bf16[1024,256]{1,0:T(8,128)(2,1)} %get-tuple-element.21) | copy-start | bytes 1572868
  9.1 4.4 %copy-start.16 = (bf16[1024,256]{1,0:T(8,128)(2,1)S(1)}, bf16[1024,256]{1,0:T(8,128)(2,1)}, u32[]{:S(2)}) copy-start(bf16[1024,256]{1,0:T(8,128)(2,1)} %get-tuple-element.20) | copy-start | bytes 1572868
  9.3 15.3 %copy-start.3 = (bf16[128,2048]{1,0:T(8,128)(2,1)}, bf16[128,2048]{1,0:T(8,128)(2,1)S(1)}, u32[]{:S(2)}) copy-start(bf16[128,2048]{1,0:T(8,128)(2,1)S(1)} %multiply_convert_fusion) | copy-start | bytes 1572868
  11.2 3.0 %copy-start.14 = (bf16[2,2048,256]{2,1,0:T(8,128)(2,1)S(1)}, bf16[2,2048,256]{2,1,0:T(8,128)(2,1)}, u32[]{:S(2)}) copy-start(bf16[2,2048,256]{2,1,0:T(8,128)(2,1)} %param.32) | copy-start | bytes 6291460
  16.8 2.7 %copy-start.9 = (bf16[2048,384]{1,0:T(8,128)(2,1)S(1)}, bf16[2048,384]{1,0:T(8,128)(2,1)}, u32[]{:S(2)}) copy-start(bf16[2048,384]{1,0:T(8,128)(2,1)} %param.39) | copy-start | bytes 4718596
  16.8 3.2 %copy-start.24 = (bf16[4,384]{1,0:T(4,128)(2,1)S(1)}, bf16[4,384]{1,0:T(4,128)(2,1)}, u32[]{:S(2)}) copy-start(bf16[4,384]{1,0:T(4,128)(2,1)} %param.42) | copy-start | bytes 9220
  16.8 3.2 %copy-start.27 = (bf16[2,3,384]{2,0,1:T(2,128)(2,1)S(1)}, bf16[2,3,384]{2,0,1:T(2,128)(2,1)}, u32[]{:S(2)}) copy-start(bf16[2,3,384]{2,0,1:T(2,128)(2,1)} %param.48) | copy-start | bytes 13828
  20.0 0.7 copy-start.7
  20.6 0.6 copy-start.17
  21.3 1.6 %copy-start.23 = (bf16[4,512]{1,0:T(4,128)(2,1)S(1)}, bf16[4,512]{1,0:T(4,128)(2,1)}, u32[]{:S(2)}) copy-start(bf16[4,512]{1,0:T(4,128)(2,1)} %param.43) | copy-start | bytes 12292
  21.3 1.6 %copy-start.26 = (bf16[2,3,512]{2,0,1:T(2,128)(2,1)S(1)}, bf16[2,3,512]{2,0,1:T(2,128)(2,1)}, u32[]{:S(2)}) copy-start(bf16[2,3,512]{2,0,1:T(2,128)(2,1)} %param.49) | copy-start | bytes 18436
  22.3 2.3 %copy-start.22 = (bf16[2048,6]{0,1:T(8,128)(2,1)S(1)}, bf16[2048,6]{0,1:T(8,128)(2,1)}, u32[]{:S(2)}) copy-start(bf16[2048,6]{0,1:T(8,128)(2,1)} %param.41) | copy-start | bytes 73732
  22.3 2.8 %copy-start.31 = (f32[6]{0:T(128)S(1)}, f32[6]{0:T(128)}, u32[]{:S(2)}) copy-start(f32[6]{0:T(128)} %param.45) | copy-start | bytes 76
  22.4 2.8 %copy-start.33 = (f32[6]{0:T(128)S(1)}, f32[6]{0:T(128)}, u32[]{:S(2)}) copy-start(f32[6]{0:T(128)} %param.44) | copy-start | bytes 76
  22.8 5.1 %copy-start.35 = (s32[8]{0:T(128)S(1)}, s32[8]{0:T(128)}, u32[]{:S(2)}) copy-start(s32[8]{0:T(128)} %param.37) | copy-start | bytes 100
  22.9 0.7 copy-start.5
  23.6 10.5 %copy-start.10 = (f32[8,3,512]{2,1,0:T(4,128)}, f32[8,3,512]{2,1,0:T(4,128)S(1)}, u32[]{:S(2)}) copy-start(f32[8,3,512]{2,1,0:T(4,128)S(1)} %copy.71) | copy-start | bytes 147460
  25.1 3.1 %copy-start.12 = (f32[8,16,6]{2,0,1:T(8,128)}, f32[8,16,6]{2,0,1:T(8,128)S(1)}, u32[]{:S(2)}) copy-start(f32[8,16,6]{2,0,1:T(8,128)S(1)} %copy.68) | copy-start | bytes 9220
  25.2 3.0 %copy-start.13 = (f32[8,16,6]{2,0,1:T(8,128)}, f32[8,16,6]{2,0,1:T(8,128)S(1)}, u32[]{:S(2)}) copy-start(f32[8,16,6]{2,0,1:T(8,128)S(1)} %fusion.92) | copy-start | bytes 9220
  28.2 5.9 %copy-start.4 = (f32[8,16,6,64]{3,2,1,0:T(8,128)S(1)}, f32[8,16,6,64]{3,2,1,0:T(8,128)}, u32[]{:S(2)}) copy-start(f32[8,16,6,64]{3,2,1,0:T(8,128)} %reshape.353) | copy-start | bytes 589828
  29.9 4.3 %copy-start.34 = (f32[6]{0:T(128)S(1)}, f32[6]{0:T(128)}, u32[]{:S(2)}) copy-start(f32[6]{0:T(128)} %param.46) | copy-start | bytes 76
  30.6 3.5 %copy-start.8 = (f32[8,16,6,64]{3,1,2,0:T(8,128)S(1)}, f32[8,16,6,64]{3,1,2,0:T(8,128)}, u32[]{:S(2)}) copy-start(f32[8,16,6,64]{3,1,2,0:T(8,128)} %convolution_bitcast_fusion) | copy-start | bytes 589828
  30.6 3.5 %copy-start.20 = (f32[8,16,6]{1,2,0:T(8,128)S(1)}, f32[8,16,6]{1,2,0:T(8,128)}, u32[]{:S(2)}) copy-start(f32[8,16,6]{1,2,0:T(8,128)} %copy.76) | copy-start | bytes 9220
  34.1 4.6 %copy-start.2 = (f32[8,6,64,256]{3,0,2,1:T(8,128)}, f32[8,6,64,256]{3,0,2,1:T(8,128)S(1)}, u32[]{:S(2)}) copy-start(f32[8,6,64,256]{3,0,2,1:T(8,128)S(1)} %fusion.31) | copy-start | bytes 9437188
  39.7 3.3 %copy-start.19 = (f32[8,16,6]{2,0,1:T(8,128)S(1)}, f32[8,16,6]{2,0,1:T(8,128)}, u32[]{:S(2)}) copy-start(f32[8,16,6]{2,0,1:T(8,128)} %get-tuple-element.22) | copy-start | bytes 9220
  44.3 6.6 %copy-start.25 = (s32[64,16]{0,1:T(8,128)S(1)}, s32[64,16]{0,1:T(8,128)}, u32[]{:S(2)}) copy-start(s32[64,16]{0,1:T(8,128)} %param.57) | copy-start | bytes 12292
  44.3 6.9 %copy-start.36 = (s32[8]{0:T(128)S(1)}, s32[8]{0:T(128)}, u32[]{:S(2)}) copy-start(s32[8]{0:T(128)} %param.37) | copy-start | bytes 100
  44.3 7.0 %copy-start.18 = (f32[8,3,384]{2,1,0:T(4,128)S(1)}, f32[8,3,384]{2,1,0:T(4,128)}, u32[]{:S(2)}) copy-start(f32[8,3,384]{2,1,0:T(4,128)} %copy-done.17) | copy-start | bytes 110596
  44.3 8.2 %copy-start.29 = (bf16[2048]{0:T(1024)(128)(2,1)S(1)}, bf16[2048]{0:T(1024)(128)(2,1)}, u32[]{:S(2)}) copy-start(bf16[2048]{0:T(1024)(128)(2,1)} %param.51) | copy-start | bytes 12292
  44.3 8.2 %copy-start.30 = (bf16[2048]{0:T(1024)(128)(2,1)S(1)}, bf16[2048]{0:T(1024)(128)(2,1)}, u32[]{:S(2)}) copy-start(bf16[2048]{0:T(1024)(128)(2,1)} %param.55) | copy-start | bytes 12292
  114.8 2.1 %copy-start.6 = (f32[8,16,512]{2,1,0:T(8,128)S(1)}, f32[8,16,512]{2,1,0:T(8,128)}, u32[]{:S(2)}) copy-start(f32[8,16,512]{2,1,0:T(8,128)} %copy-done.5) | copy-start | bytes 786436
  114.8 2.1 %copy-start.11 = (f32[8,3,512]{2,1,0:T(4,128)S(1)}, f32[8,3,512]{2,1,0:T(4,128)}, u32[]{:S(2)}) copy-start(f32[8,3,512]{2,1,0:T(4,128)} %copy-done.10) | copy-start | bytes 147460

commit v2 on v1

--- a/solution.py
+++ b/solution.py
@@ -29,12 +29,296 @@
     return widened * lax.rsqrt(spread + eps_norm) * gain.astype(jnp.float32)
 
 
-def convolve(series, kernel, length):
-    summed = jnp.zeros(series.shape[:-2] + (length, series.shape[-1]), jnp.float32)
-    for kernel_tap in range(kernel.shape[0]):
-        window = lax.slice_in_dim(series, kernel_tap, kernel_tap + length, axis=series.ndim - 2)
-        summed = summed + window * kernel[kernel_tap].astype(jnp.float32)
-    return jax.nn.silu(summed)
+def dot(a, b):
+    return jnp.dot(a, b, preferred_element_type=jnp.float32)
+
+
+def dot_rows(a, b):
+    return lax.dot_general(a, b, (((1,), (1,)), ((), ())), preferred_element_type=jnp.float32)
+
+
+def dot_exact(a, b):
+    return jnp.dot(
+        a, b, preferred_element_type=jnp.float32, precision=lax.Precision.HIGHEST
+    )
+
+
+def ones_where(mask, dtype=jnp.bfloat16):
+    return jnp.where(mask, 1.0, 0.0).astype(dtype)
+
+
+def mixer_kernel(
+    m,
+    member_ref,
+    lengths_ref,
+    accepted_ref,
+    hidden_ref,
+    gain_ref,
+    w_dt_ref,
+    conv_x_ref,
+    conv_bc_ref,
+    rows_x_ref,
+    rows_bc_ref,
+    head_params_ref,
+    w_query_hbm,
+    w_kv_hbm,
+    prompt_kv_hbm,
+    w_z_hbm,
+    w_x_hbm,
+    w_bc_hbm,
+    state_hbm,
+    w_attn_hbm,
+    w_mamba_hbm,
+    mixed_ref,
+    kept_ref,
+    edge_x_ref,
+    edge_bc_ref,
+    w_query,
+    w_kv,
+    prompt_kv,
+    w_z,
+    w_x,
+    w_bc,
+    state,
+    w_attn,
+    w_mamba,
+    normed_ref,
+    load_sems,
+):
+    mdl = lax.axis_index("mdl")
+    local_heads = w_query.shape[1] // HEAD_DIM
+    group = mdl * local_heads // (Q_HEADS // KV_HEADS)
+    pairs = (
+        (w_x_hbm, w_x),
+        (w_bc_hbm, w_bc),
+        (w_z_hbm, w_z),
+        (w_query_hbm, w_query),
+        (w_kv_hbm.at[group], w_kv),
+        (state_hbm, state),
+        (prompt_kv_hbm.at[:, group], prompt_kv),
+        (w_attn_hbm, w_attn),
+        (w_mamba_hbm, w_mamba),
+    )
+    loads = [
+        pltpu.make_async_copy(src, dst, load_sems.at[i]) for i, (src, dst) in enumerate(pairs)
+    ]
+    for load in loads:
+        load.start()
+
+    tokens, width = hidden_ref.shape
+    reqs = tokens // DRAFT
+    inner = w_x.shape[1]
+    heads = inner // SSM_DIM
+    edge = CONV - 1
+    bf16, f32 = jnp.bfloat16, jnp.float32
+    token = lax.broadcasted_iota(jnp.int32, (tokens, 1), 0)
+    request, position = token // DRAFT, token % DRAFT
+    other = lax.broadcasted_iota(jnp.int32, (1, tokens), 1)
+    other_request, other_position = other // DRAFT, other % DRAFT
+    member = jnp.zeros((tokens, 1), jnp.int32)
+    accepted = jnp.zeros((tokens, 1), jnp.int32)
+    for r in range(reqs):
+        member = jnp.where(request == r, member_ref[r], member)
+        accepted = jnp.where(request == r, accepted_ref[r], accepted)
+    first_prompt = member == 0
+    valid = jnp.where(first_prompt, lengths_ref[0], lengths_ref[1])
+    same = request == other_request
+    causal = same & (other_position <= position)
+
+    normed_ref[...] = rms_scale(hidden_ref[...], gain_ref[...]).astype(bf16)
+    normed = normed_ref[...]
+    dt_in = dot(normed, w_dt_ref[...]).astype(bf16)
+    loads[0].wait()
+    ssm_in = dot(normed, w_x[...]).astype(bf16)
+    loads[1].wait()
+    bc_in = dot(normed, w_bc[...]).astype(bf16)
+
+    row_at = lax.broadcasted_iota(jnp.int32, (1, rows_x_ref.shape[0]), 1)
+    rows_x, rows_bc = rows_x_ref[...], rows_bc_ref[...]
+    keep = position < edge
+    kept_at = accepted + position
+    pick_drafts = ones_where(same & keep & (other_position == kept_at - edge))
+    pick_prompt = ones_where((row_at == member * edge + kept_at) & (kept_at < edge) & keep)
+    edge_x_ref[...] = (dot(pick_drafts, ssm_in) + dot(pick_prompt, rows_x)).astype(bf16)
+    edge_bc_ref[...] = (dot(pick_drafts, bc_in) + dot(pick_prompt, rows_bc)).astype(bf16)
+
+    def convolved(series, rows, taps):
+        wide = series.astype(f32)
+        total = wide * taps[edge : edge + 1].astype(f32)
+        for back in range(1, CONV):
+            shifted = jnp.where(position >= back, pltpu.roll(wide, back, 0), 0.0)
+            begin = ones_where(
+                (row_at == member * edge + edge + position - back) & (position < back)
+            )
+            shifted = shifted + dot(begin, rows)
+            total = total + shifted * taps[edge - back : edge - back + 1].astype(f32)
+        return jax.nn.silu(total)
+
+    x = convolved(ssm_in, rows_x, conv_x_ref[...])
+    bc = convolved(bc_in, rows_bc, conv_bc_ref[...])
+    b_part = bc[:, :STATE].astype(bf16)
+    c_part = bc[:, STATE:].astype(bf16)
+
+    head_row = lax.broadcasted_iota(jnp.int32, (dt_in.shape[1], inner), 0)
+    head_col = lax.broadcasted_iota(jnp.int32, (dt_in.shape[1], inner), 1)
+    spread = ones_where(head_row == head_col // SSM_DIM)
+    dt_bias = head_params_ref[0:1, :]
+    rate = head_params_ref[1:2, :]
+    skip = head_params_ref[2:3, :]
+    raw = dot(dt_in, spread) + dt_bias
+    step_size = jnp.maximum(raw, 0.0) + jnp.log1p(jnp.exp(-jnp.abs(raw)))
+    log_decay = dot_exact(ones_where(causal, f32), -step_size * rate)
+    log_rows = log_decay.T
+    last = accepted - 1
+    final_log = dot_exact(ones_where(same & (other_position == last), f32), log_decay)
+    final_rows = jnp.exp(final_log.T)
+    carry = jnp.exp(jnp.where(position <= last, final_log - log_decay, far_below)) * step_size
+    carried_t = (carry * x).T.astype(bf16)
+
+    loads[5].wait()
+    flat = (inner, STATE)
+    first_state, second_state = state[0].reshape(flat), state[1].reshape(flat)
+    for r in range(reqs):
+        own = jnp.where(request == r, b_part, jnp.zeros_like(b_part))
+        begin = jnp.where(
+            jnp.broadcast_to(member_ref[r], (1, STATE)) == 0, first_state, second_state
+        )
+        kept = final_rows[:, r * DRAFT : r * DRAFT + 1] * begin + dot(carried_t, own)
+        kept_ref[r] = kept.astype(bf16).reshape(heads, SSM_DIM, STATE)
+
+    initial = jnp.where(
+        first_prompt,
+        dot_rows(c_part, first_state.astype(bf16)),
+        dot_rows(c_part, second_state.astype(bf16)),
+    )
+    overlap = dot_rows(c_part, b_part)
+    stepped = (step_size * x).astype(bf16)
+    intra = []
+    for h in range(heads):
+        at = h * SSM_DIM
+        gaps = log_decay[:, at : at + 1] - log_rows[at : at + 1, :]
+        mixing = jnp.exp(jnp.where(causal, gaps, far_below)) * overlap
+        intra.append(dot(mixing.astype(bf16), stepped[:, at : at + SSM_DIM]))
+    ssm_out = jnp.concatenate(intra, axis=1) + initial * jnp.exp(log_decay) + skip * x
+    loads[2].wait()
+    gate_z = dot(normed, w_z[...]).astype(bf16).astype(f32)
+    gated = (ssm_out * jax.nn.silu(gate_z)).astype(bf16)
+
+    loads[3].wait()
+    queries = dot(normed, w_query[...]).astype(bf16)
+    loads[4].wait()
+    key_value = dot(normed, w_kv[...]).astype(bf16)
+    loads[6].wait()
+    scale = HEAD_DIM ** (-0.5)
+    usable = lax.broadcasted_iota(jnp.int32, (1, P_MAX), 1) < valid
+    attended = []
+    for h in range(local_heads):
+        query = queries[:, h * HEAD_DIM : (h + 1) * HEAD_DIM]
+        scores = jnp.where(
+            first_prompt,
+            dot_rows(query, prompt_kv[0, :, :HEAD_DIM]),
+            dot_rows(query, prompt_kv[1, :, :HEAD_DIM]),
+        )
+        scores = jnp.where(usable, scores * scale, far_below)
+        drafts = jnp.where(causal, dot_rows(query, key_value[:, :HEAD_DIM]) * scale, far_below)
+        top = jnp.maximum(
+            jnp.max(scores, axis=1, keepdims=True), jnp.max(drafts, axis=1, keepdims=True)
+        )
+        weights = jnp.exp(scores - top)
+        draft_weights = jnp.exp(drafts - top)
+        denominator = jnp.sum(weights, axis=1, keepdims=True) + jnp.sum(
+            draft_weights, axis=1, keepdims=True
+        )
+        rounded = weights.astype(bf16)
+        summed = jnp.where(
+            first_prompt,
+            dot(rounded, prompt_kv[0, :, HEAD_DIM:]),
+            dot(rounded, prompt_kv[1, :, HEAD_DIM:]),
+        ) + dot(draft_weights.astype(bf16), key_value[:, HEAD_DIM:])
+        attended.append((summed / denominator).astype(bf16))
+    attended = jnp.concatenate(attended, axis=1)
+    loads[7].wait()
+    loads[8].wait()
+    for first in range(0, width, 512):
+        at = slice(first, first + 512)
+        mixed_ref[:, at] = (dot(attended, w_attn[:, at]) + dot(gated, w_mamba[:, at])).astype(bf16)
+
+
+def run_mixers(
+    member,
+    lengths,
+    accepted,
+    hidden,
+    gain,
+    w_dt,
+    conv_x,
+    conv_bc,
+    rows_x,
+    rows_bc,
+    head_params,
+    w_query,
+    w_kv,
+    prompt_kv,
+    w_z,
+    w_x,
+    w_bc,
+    state,
+    w_attn,
+    w_mamba,
+):
+    m = lax.axis_size("mdl")
+    tokens, width = hidden.shape
+    reqs = tokens // DRAFT
+    smem = pl.BlockSpec(memory_space=pltpu.SMEM)
+    vmem = pl.BlockSpec(memory_space=pltpu.VMEM)
+    anywhere = pl.BlockSpec(memory_space=pl.ANY)
+    bf16 = jnp.bfloat16
+    return pl.pallas_call(
+        functools.partial(mixer_kernel, m),
+        out_shape=(
+            jax.ShapeDtypeStruct((tokens, width), bf16),
+            jax.ShapeDtypeStruct((reqs,) + state.shape[1:], bf16),
+            jax.ShapeDtypeStruct((tokens, w_x.shape[1]), bf16),
+            jax.ShapeDtypeStruct((tokens, w_bc.shape[1]), bf16),
+        ),
+        in_specs=[smem] * 3 + [vmem] * 8 + [anywhere] * 9,
+        out_specs=(vmem,) * 4,
+        scratch_shapes=[
+            pltpu.VMEM(w_query.shape, bf16),
+            pltpu.VMEM(w_kv.shape[1:], bf16),
+            pltpu.VMEM((PROMPTS,) + prompt_kv.shape[2:], bf16),
+            pltpu.VMEM(w_z.shape, bf16),
+            pltpu.VMEM(w_x.shape, bf16),
+            pltpu.VMEM(w_bc.shape, bf16),
+            pltpu.VMEM(state.shape, jnp.float32),
+            pltpu.VMEM(w_attn.shape, bf16),
+            pltpu.VMEM(w_mamba.shape, bf16),
+            pltpu.VMEM((tokens, width), bf16),
+            pltpu.SemaphoreType.DMA((9,)),
+        ],
+        compiler_params=pltpu.CompilerParams(vmem_limit_bytes=40 * 1024 * 1024),
+    )(
+        member,
+        lengths,
+        accepted,
+        hidden,
+        gain,
+        w_dt,
+        conv_x,
+        conv_bc,
+        rows_x,
+        rows_bc,
+        head_params,
+        w_query,
+        w_kv,
+        prompt_kv,
+        w_z,
+        w_x,
+        w_bc,
+        state,
+        w_attn,
+        w_mamba,
+    )
 
 
 def tail_kernel(
@@ -412,157 +696,38 @@
     row_tokens = row_reqs * draft_len
     own_reqs = row_reqs // mdl_count
     own_tokens = own_reqs * draft_len
-    contract_last = (((1,), (1,)), ((), ()))
     flat_rows = hidden_in.reshape(row_tokens, width)
-    normed = rms_scale(flat_rows, mixer_gain).astype(jnp.bfloat16)
-    token_request = jnp.arange(row_tokens) // draft_len
-    token_position = jnp.arange(row_tokens) % draft_len
-    prompt_pick = jax.nn.one_hot(member, PROMPTS, dtype=jnp.float32)
-    local_heads = w_query.shape[1] // HEAD_DIM
-    per_group = Q_HEADS // KV_HEADS
-    kv_index = mdl_rank * local_heads // per_group
-    kv_weight = lax.dynamic_index_in_dim(w_kv, kv_index, 0, keepdims=False)
-    queries = jnp.dot(normed, w_query, preferred_element_type=jnp.float32).astype(jnp.bfloat16)
-    key_value = jnp.dot(normed, kv_weight, preferred_element_type=jnp.float32).astype(jnp.bfloat16)
-    draft_keys = key_value[:, :HEAD_DIM]
-    draft_values = key_value[:, HEAD_DIM:]
-    query_rows = (
-        queries.reshape(row_tokens, local_heads, HEAD_DIM)
-        .transpose(1, 0, 2)
-        .reshape(local_heads * row_tokens, HEAD_DIM)
-    )
-    row_request = jnp.tile(token_request, local_heads)
-    row_position = jnp.tile(token_position, local_heads)
-    row_member = jnp.take(member, row_request)
-    cached = lax.dynamic_index_in_dim(prompt_kv, kv_index, 1, keepdims=False)
-    score_scale = HEAD_DIM ** (-0.5)
-    draft_scores = (
-        lax.dot_general(query_rows, draft_keys, contract_last, preferred_element_type=jnp.float32)
-        * score_scale
-    )
-    draft_mask = (row_request[:, None] == token_request[None, :]) & (
-        token_position[None, :] <= row_position[:, None]
-    )
-    draft_top = jnp.max(jnp.where(draft_mask, draft_scores, far_below), axis=1)
-
-    def prompt_scores(prompt_slot, row_count):
-        key_block = cached[prompt_slot]
-        scores = (
-            lax.dot_general(
-                query_rows,
-                key_block[:, :HEAD_DIM],
-                contract_last,
-                preferred_element_type=jnp.float32,
-            )
-            * score_scale
-        )
-        positions = jnp.arange(row_count)
-        valid_keys = (row_member[:, None] == prompt_slot) & (
-            positions[None, :] < prompt_lengths[prompt_slot]
-        )
-        return (scores, valid_keys, key_block[:, HEAD_DIM:])
-
-    def add_weights(carry, scores, valid_keys, values_block, row_top):
-        weight_total, weighted = carry
-        weights = jnp.exp(jnp.where(valid_keys, scores - row_top[:, None], far_below))
-        weight_total = weight_total + jnp.sum(weights, axis=1)
-        weighted = weighted + jnp.dot(
-            weights.astype(jnp.bfloat16), values_block, preferred_element_type=jnp.float32
-        )
-        return (weight_total, weighted)
-
-    row_top = draft_top
-    prompt_parts = []
-    for prompt_slot in range(PROMPTS):
-        scores, valid_keys, values_block = prompt_scores(prompt_slot, P_MAX)
-        row_top = jnp.maximum(row_top, jnp.max(jnp.where(valid_keys, scores, far_below), axis=1))
-        prompt_parts.append((scores, valid_keys, values_block))
-    carry = (
-        jnp.zeros(row_top.shape, jnp.float32),
-        jnp.zeros((query_rows.shape[0], HEAD_DIM), jnp.float32),
-    )
-    for scores, valid_keys, values_block in prompt_parts:
-        carry = add_weights(carry, scores, valid_keys, values_block, row_top)
-    carry = add_weights(carry, draft_scores, draft_mask, draft_values, row_top)
-    attended = (carry[1] / carry[0][:, None]).astype(jnp.bfloat16)
-    attention_flat = (
-        attended.reshape(local_heads, row_tokens, HEAD_DIM)
-        .transpose(1, 0, 2)
-        .reshape(row_tokens, local_heads * HEAD_DIM)
-    )
-    gate_z = jnp.dot(normed, w_z, preferred_element_type=jnp.float32).astype(jnp.bfloat16)
-    ssm_in = jnp.dot(normed, w_x, preferred_element_type=jnp.float32).astype(jnp.bfloat16)
-    bc_in = jnp.dot(normed, w_bc, preferred_element_type=jnp.float32).astype(jnp.bfloat16)
-    dt_in = jnp.dot(normed, w_dt, preferred_element_type=jnp.float32).astype(jnp.bfloat16)
+    edge_len = CONV - 1
     local_inner = w_x.shape[1]
-    local_ssm = local_inner // SSM_DIM
-    edge_len = CONV - 1
-    start_x = jnp.einsum(
-        "rp,pcw->rcw",
-        prompt_pick,
-        prompt_conv_x.astype(jnp.float32),
-        precision=lax.Precision.HIGHEST,
-    )
-    start_bc = jnp.einsum(
-        "rp,pcw->rcw",
-        prompt_pick,
-        prompt_conv_bc.astype(jnp.float32),
-        precision=lax.Precision.HIGHEST,
-    )
-    series_x = jnp.concatenate(
-        [start_x, ssm_in.astype(jnp.float32).reshape(row_reqs, draft_len, local_inner)], axis=1
-    )
-    series_bc = jnp.concatenate(
-        [start_bc, bc_in.astype(jnp.float32).reshape(row_reqs, draft_len, 2 * STATE)], axis=1
-    )
-    conv_xs = convolve(series_x, conv_x, draft_len)
-    conv_bcs = convolve(series_bc, conv_bc, draft_len)
-    b_part = conv_bcs[:, :, :STATE]
-    c_part = conv_bcs[:, :, STATE:]
-    step_size = jax.nn.softplus(
-        dt_in.astype(jnp.float32).reshape(row_reqs, draft_len, local_ssm) + dt_bias
-    )
-    log_decay = jnp.cumsum(-step_size * ssm_rate, axis=1)
-    heads_x = conv_xs.reshape(row_reqs, draft_len, local_ssm, SSM_DIM)
-    causal_pairs = jnp.arange(draft_len)[:, None] >= jnp.arange(draft_len)[None, :]
-    log_gaps = log_decay[:, :, None, :] - log_decay[:, None, :, :]
-    mixing = jnp.exp(jnp.where(causal_pairs[None, :, :, None], log_gaps, far_below))
-    intersection = jnp.einsum("rtn,rsn->rts", c_part, b_part, precision=lax.Precision.HIGHEST)
-    pair_weights = mixing * intersection[..., None] * step_size[:, None, :, :]
-    intra = jnp.einsum("rtsh,rshp->rthp", pair_weights, heads_x, precision=lax.Precision.HIGHEST)
-    initial = jnp.einsum(
-        "rp,phdn->rhdn", prompt_pick, prompt_state, precision=lax.Precision.HIGHEST
-    )
-    carried = (
-        jnp.einsum("rhdn,rtn->rthd", initial, c_part, precision=lax.Precision.HIGHEST)
-        * jnp.exp(log_decay)[..., None]
-    )
-    ssm_out = intra + carried + skip_d[None, None, :, None] * heads_x
-    gated = (
-        ssm_out.reshape(row_tokens, local_inner) * jax.nn.silu(gate_z.astype(jnp.float32))
-    ).astype(jnp.bfloat16)
-    last_index = accepted - 1
-    pick_step = jax.nn.one_hot(last_index, draft_len, dtype=jnp.float32)
-    final_log = jnp.einsum("rt,rth->rh", pick_step, log_decay, precision=lax.Precision.HIGHEST)
-    upto_last = jnp.arange(draft_len)[None, :] <= last_index[:, None]
-    carry_weights = (
-        jnp.exp(jnp.where(upto_last[:, :, None], final_log[:, None, :] - log_decay, far_below))
-        * step_size
-    )
-    kept_states = jnp.exp(final_log)[:, :, None, None] * initial
-    kept_states = kept_states + jnp.einsum(
-        "rsh,rshd,rsn->rhdn", carry_weights, heads_x, b_part, precision=lax.Precision.HIGHEST
-    )
-    window_pick = jax.nn.one_hot(
-        accepted[:, None] + jnp.arange(edge_len)[None, :], edge_len + draft_len, dtype=jnp.float32
-    )
-    kept_x = jnp.einsum("rkl,rlc->rkc", window_pick, series_x, precision=lax.Precision.HIGHEST)
-    kept_bc = jnp.einsum("rkl,rlc->rkc", window_pick, series_bc, precision=lax.Precision.HIGHEST)
-    edges = jnp.pad(kept_x.astype(jnp.bfloat16), ((0, 0), (0, 16 - edge_len), (0, 0)))
-    mixed = (
-        jnp.dot(attention_flat, w_attn_out, preferred_element_type=jnp.float32)
-        + jnp.dot(gated, w_mamba_out, preferred_element_type=jnp.float32)
-    ).astype(jnp.bfloat16)
+
+    def edge_rows(rows):
+        rows = rows.reshape(PROMPTS * edge_len, rows.shape[2])
+        return jnp.pad(rows, ((0, 16 - PROMPTS * edge_len), (0, 0)))
+
+    mixed, kept_states, edge_x_rows, edge_bc_rows = run_mixers(
+        member,
+        prompt_lengths,
+        accepted,
+        flat_rows,
+        mixer_gain.reshape(1, width),
+        w_dt,
+        conv_x,
+        conv_bc,
+        edge_rows(prompt_conv_x),
+        edge_rows(prompt_conv_bc),
+        jnp.repeat(jnp.stack([dt_bias, ssm_rate, skip_d]), SSM_DIM, axis=1),
+        w_query,
+        w_kv,
+        prompt_kv,
+        w_z,
+        w_x,
+        w_bc,
+        prompt_state,
+        w_attn_out,
+        w_mamba_out,
+    )
+    edges = edge_x_rows.reshape(row_reqs, draft_len, local_inner)
+    kept_bc = edge_bc_rows.reshape(row_reqs, draft_len, 2 * STATE)[:, :edge_len]
     id_grid = draft_ids.reshape(req_count, mdl_count, own_reqs, draft_len)
     column_ids = lax.dynamic_index_in_dim(id_grid, mdl_rank, 1, keepdims=False)
     next_ids = jnp.concatenate([column_ids[..., 1:], column_ids[..., :1]], axis=-1).reshape(1, -1)
@@ -576,7 +741,7 @@
         w_up,
         w_down,
         head_weight,
-        kept_states.astype(jnp.bfloat16),
+        kept_states,
         edges,
     )
     kept_state = kept_all.astype(jnp.float32)
@@ -586,7 +751,7 @@
         .reshape(own_reqs, edge_len, mdl_count * local_inner)
     )
     own_bc = lax.dynamic_slice_in_dim(kept_bc, mdl_rank * own_reqs, own_reqs, 0)
-    kept_conv = jnp.concatenate([edge_x, own_bc.astype(jnp.bfloat16)], axis=2)
+    kept_conv = jnp.concatenate([edge_x, own_bc], axis=2)
     verify_scores = lax.dynamic_slice_in_dim(
         scores_all[0], req_rank * own_tokens, own_tokens, 0
     ).reshape(own_reqs, draft_len)

time: 121 us -> 98.3 us (0.81)
  matrix products: 31.3 us -> 0 us
  local copies, waits for them, and re-layouts: 10.5 us -> 22.1 us
  other arithmetic: 13.9 us -> 3.47 us
  Pallas kernels: 62.2 us -> 70.5 us
    dot_general x23 -> x0, matrix products: 31.3 us -> none  [the longest x1 6.53 us: shards(): jnp.einsum('rsh,rshd,rsn->rhdn', carry_weights, heads_x, b_part, precisio...]
    unnamed x77 -> x36, local copies, waits for them, and re-layouts: 2.38 us -> 18.8 us
    pallas_call x0 -> x1, Pallas kernels: none -> 8.36 us  [run_mixers(): pl.pallas_call(functools.partial(mixer_kernel, m), out_shape=(jax.ShapeDt...]
    gather x2 -> x0, other arithmetic: 4.36 us -> none  [shards(): row_member = jnp.take(member, row_request)]
    squeeze x1 -> x0, local copies, waits for them, and re-layouts: 2.39 us -> none  [prompt_scores(): key_block = cached[prompt_slot]]
    mul x3 -> x0, other arithmetic: 2.01 us -> none  [the longest x1 1.65 us: shards(): jnp.exp(jnp.where(upto_last[:, :, None], final_log[:, None, :] - log_deca...]
    lt x1 -> x0, other arithmetic: 1.33 us -> none  [prompt_scores(): positions[None, :] < prompt_lengths[prompt_slot]]
    reshape x6 -> x4, local copies, waits for them, and re-layouts: 2.09 us -> 0.81 us  [the longest x1 0.69 us: shards(): mixer_gain.reshape(1, width)]
where the time goes in v2:
time: 98.3 us; the launch traced here: 96.8 us
  Pallas kernels  70.5 us (72%)
  local copies, waits for them, and re-layouts  22.1 us (22%)
  other arithmetic  3.47 us (4%)
    pallas_call x1, Pallas kernels, run_tail(): pl.pallas_call(functools.partial(tail_kernel, n, m), out_shape=(jax.Shape...  62.1 us
    unnamed x36, local copies, waits for them, and re-layouts  18.8 us
    pallas_call x1, Pallas kernels, run_mixers(): pl.pallas_call(functools.partial(mixer_kernel, m), out_shape=(jax.ShapeDt...  8.36 us
    convert_element_type x1, other arithmetic, shards(): kept_state = kept_all.astype(jnp.float32)  2.06 us

profile of v2, /device:TPU:9, one launch (start us, length us, event | category | flops | bytes accessed | tf_op | source)
XLA Modules:
  0.0 96.8 jit_solution(13940472577053934928)
XLA Ops:
  0.6 0.7 pad_maximum_fusion.1
  1.3 0.7 copy.37
  2.1 0.7 reshape.52.gain_ref
  2.8 0.7 copy.38
  3.5 0.7 reshape.56.mlp_gain_ref
  4.2 0.7 reshape.57.final_gain_ref
  4.9 0.1 broadcast_in_dim.10
  4.9 0.1 reshape.55.head_params_ref
  5.0 0.8 copy.40
  5.8 0.1 slice.20
  5.9 0.1 pad_add_fusion
  6.0 0.1 broadcast_in_dim.11
  6.1 1.1 %copy.39.w_dt_ref = bf16[2048,6]{1,0:T(8,128)(2,1)S(1)} copy(bf16[2048,6]{0,1:T(8,128)(2,1)} %param.41) | data formatting | bytes 49152 | tf_op args[12]
  7.1 0.0 copy-start
  7.1 1.6 %copy-done = bf16[2,2048,256]{2,1,0:T(8,128)(2,1)S(1)} copy-done((bf16[2,2048,256]{2,1,0:T(8,128)(2,1)S(1)}, bf16[2,2048,256]{2,1,0:T(8,128)(2,1)}, u32[]{:S(2)}) %copy-start) | copy-done | bytes 2097176
  8.7 0.0 copy-start.1
  8.7 1.0 %copy-done.1 = bf16[8,16,2048]{2,1,0:T(8,128)(2,1)S(1)} copy-done((bf16[8,16,2048]{2,1,0:T(8,128)(2,1)S(1)}, bf16[8,16,2048]{2,1,0:T(8,128)(2,1)}, u32[]{:S(2)}) %copy-start.1) | copy-done | bytes 524312
  9.8 0.0 copy-start.3
  9.8 1.4 %copy-done.3 = bf16[2048,384]{1,0:T(8,128)(2,1)S(1)} copy-done((bf16[2048,384]{1,0:T(8,128)(2,1)S(1)}, bf16[2048,384]{1,0:T(8,128)(2,1)}, u32[]{:S(2)}) %copy-start.3) | copy-done | bytes 1572888
  11.2 0.0 copy-start.4
  11.2 1.4 %copy-done.4 = bf16[2048,384]{1,0:T(8,128)(2,1)S(1)} copy-done((bf16[2048,384]{1,0:T(8,128)(2,1)S(1)}, bf16[2048,384]{1,0:T(8,128)(2,1)}, u32[]{:S(2)}) %copy-start.4) | copy-done | bytes 1572888
  12.6 0.0 copy-start.5
  12.6 1.4 %copy-done.5 = bf16[384,2048]{1,0:T(8,128)(2,1)S(1)} copy-done((bf16[384,2048]{1,0:T(8,128)(2,1)S(1)}, bf16[384,2048]{1,0:T(8,128)(2,1)}, u32[]{:S(2)}) %copy-start.5) | copy-done | bytes 1572888
  14.0 1.2 %copy-done.7 = bf16[2048,256]{1,0:T(8,128)(2,1)S(1)} copy-done((bf16[2048,256]{1,0:T(8,128)(2,1)S(1)}, bf16[2048,256]{1,0:T(8,128)(2,1)}, u32[]{:S(2)}) %copy-start.7) | copy-done | bytes 1048600
  15.2 0.0 copy-start.8
  15.2 1.2 %copy-done.8 = bf16[256,2048]{1,0:T(8,128)(2,1)S(1)} copy-done((bf16[256,2048]{1,0:T(8,128)(2,1)S(1)}, bf16[256,2048]{1,0:T(8,128)(2,1)}, u32[]{:S(2)}) %copy-start.8) | copy-done | bytes 1048600
  16.4 0.0 copy-start.9
  16.4 1.1 %copy-done.9 = f32[2,6,64,256]{3,2,1,0:T(8,128)S(1)} copy-done((f32[2,6,64,256]{3,2,1,0:T(8,128)S(1)}, f32[2,6,64,256]{3,2,1,0:T(8,128)}, u32[]{:S(2)}) %copy-start.9) | copy-done | bytes 786456
  17.6 0.0 copy-start.10
  17.6 0.7 copy-done.10
  18.3 0.0 copy-start.11
  18.3 0.7 copy-done.11
  19.0 0.0 copy-start.12
  19.0 0.7 copy-done.12
  19.6 0.0 copy-start.13
  19.6 0.7 copy-done.13
  20.3 0.0 copy-start.14
  20.3 0.7 copy-done.14
  20.9 8.4 %shard_map.300 = (bf16[128,2048]{1,0:T(8,128)(2,1)S(1)}, bf16[8,6,64,256]{3,2,1,0:T(8,128)(2,1)S(1)}, bf16[128,384]{1,0:T(8,128)(2,1)S(1)}, bf16[128,512]{1,0:T(8,128)(2,1)S(1)}) custom-call(s32[8]{0:T(128)S(1)} %copy-done.12, s32[2]{0:T(128)S(1)} %copy-done.13, s32[8]{0:T(128)S(1)} %copy-done.14, bf16[128,2048]{1,0:T(8,128)(2,1)S(1)} %bitcast.15, ...), custom_call_target="tpu_custom_call" | custom-call | tf_op jit(solution)/shard_map/pallas_call | solution.py:276
  29.3 0.0 copy-start.6
  29.3 1.1 %copy-done.6 = bf16[8,6,64,256]{3,2,1,0:T(8,128)(2,1)} copy-done((bf16[8,6,64,256]{3,2,1,0:T(8,128)(2,1)}, bf16[8,6,64,256]{3,2,1,0:T(8,128)(2,1)S(1)}, u32[]{:S(2)}) %copy-start.6) | copy-done | bytes 1572888
  30.4 0.0 copy-done.2
  30.4 62.1 %shard_map.301 = (bf16[32,2048]{1,0:T(8,128)(2,1)S(1)}, f32[8,256]{1,0:T(8,128)S(1)}, bf16[2,24,64,256]{3,2,1,0:T(8,128)(2,1)S(1)}, bf16[4,2,16,384]{3,2,1,0:T(8,128)(2,1)S(1)}) custom-call(bf16[128,2048]{1,0:T(8,128)(2,1)S(1)} %get-tuple-element.12.mixed_ref, bf16[128,2048]{1,0:T(8,128)(2,1)S(1)} %bitcast.16, bf16[1,2048]{1,0:T(2,128)(2,1)S(1)} %reshape.56.mlp_gain_ref, ...), custom_call_target="tpu_custom_call" | custom-call | tf_op jit(solution)/shard_map/pallas_call | solution.py:618
  92.6 0.1 fusion
  92.7 0.6 reshape.61
  93.4 0.6 pad_maximum_fusion
  94.1 2.1 %convert_element_type.7 = f32[2,24,64,256]{3,2,1,0:T(8,128)} convert(bf16[2,24,64,256]{3,2,1,0:T(8,128)(2,1)S(1)} %get-tuple-element.17) | non-fusion elementwise | flops 786432 | bytes 4718592 | tf_op jit(solution)/shard_map/convert_element_type | solution.py:747
  96.1 0.7 copy.46
  (15 shorter events, 0.1 us)
Async XLA Ops:
  7.1 1.6 %copy-start = (bf16[2,2048,256]{2,1,0:T(8,128)(2,1)S(1)}, bf16[2,2048,256]{2,1,0:T(8,128)(2,1)}, u32[]{:S(2)}) copy-start(bf16[2,2048,256]{2,1,0:T(8,128)(2,1)} %w_kv_hbm.1) | copy-start | bytes 6291460
  8.7 1.0 %copy-start.1 = (bf16[8,16,2048]{2,1,0:T(8,128)(2,1)S(1)}, bf16[8,16,2048]{2,1,0:T(8,128)(2,1)}, u32[]{:S(2)}) copy-start(bf16[8,16,2048]{2,1,0:T(8,128)(2,1)} %param.29) | copy-start | bytes 1572868
  9.8 1.4 %copy-start.3 = (bf16[2048,384]{1,0:T(8,128)(2,1)S(1)}, bf16[2048,384]{1,0:T(8,128)(2,1)}, u32[]{:S(2)}) copy-start(bf16[2048,384]{1,0:T(8,128)(2,1)} %w_z_hbm.1) | copy-start | bytes 4718596
  11.2 1.4 %copy-start.4 = (bf16[2048,384]{1,0:T(8,128)(2,1)S(1)}, bf16[2048,384]{1,0:T(8,128)(2,1)}, u32[]{:S(2)}) copy-start(bf16[2048,384]{1,0:T(8,128)(2,1)} %w_x_hbm.1) | copy-start | bytes 4718596
  12.6 1.4 %copy-start.5 = (bf16[384,2048]{1,0:T(8,128)(2,1)S(1)}, bf16[384,2048]{1,0:T(8,128)(2,1)}, u32[]{:S(2)}) copy-start(bf16[384,2048]{1,0:T(8,128)(2,1)} %w_mamba_hbm.1) | copy-start | bytes 4718596
  14.0 1.2 %copy-start.7 = (bf16[2048,256]{1,0:T(8,128)(2,1)S(1)}, bf16[2048,256]{1,0:T(8,128)(2,1)}, u32[]{:S(2)}) copy-start(bf16[2048,256]{1,0:T(8,128)(2,1)} %w_query_hbm.1) | copy-start | bytes 3145732
  15.2 1.2 %copy-start.8 = (bf16[256,2048]{1,0:T(8,128)(2,1)S(1)}, bf16[256,2048]{1,0:T(8,128)(2,1)}, u32[]{:S(2)}) copy-start(bf16[256,2048]{1,0:T(8,128)(2,1)} %w_attn_hbm.1) | copy-start | bytes 3145732
  16.4 1.1 %copy-start.9 = (f32[2,6,64,256]{3,2,1,0:T(8,128)S(1)}, f32[2,6,64,256]{3,2,1,0:T(8,128)}, u32[]{:S(2)}) copy-start(f32[2,6,64,256]{3,2,1,0:T(8,128)} %state_hbm.1) | copy-start | bytes 2359300
  17.6 0.7 copy-start.10
  18.3 0.7 copy-start.11
  19.0 0.7 copy-start.12
  19.6 0.7 copy-start.13
  20.3 0.7 copy-start.14
  20.9 9.5 %copy-start.2 = (bf16[8,16,2048]{2,1,0:T(8,128)(2,1)S(1)}, bf16[8,16,2048]{2,1,0:T(8,128)(2,1)}, u32[]{:S(2)}) copy-start(bf16[8,16,2048]{2,1,0:T(8,128)(2,1)} %param.29) | copy-start | bytes 1572868
  29.3 1.1 %copy-start.6 = (bf16[8,6,64,256]{3,2,1,0:T(8,128)(2,1)}, bf16[8,6,64,256]{3,2,1,0:T(8,128)(2,1)S(1)}, u32[]{:S(2)}) copy-start(bf16[8,6,64,256]{3,2,1,0:T(8,128)(2,1)S(1)} %get-tuple-element.13.kept_hbm) | copy-start | bytes 4718596

commit v3 on v2

--- a/solution.py
+++ b/solution.py
@@ -59,7 +59,9 @@
     conv_bc_ref,
     rows_x_ref,
     rows_bc_ref,
-    head_params_ref,
+    dt_bias_ref,
+    rate_ref,
+    skip_ref,
     w_query_hbm,
     w_kv_hbm,
     prompt_kv_hbm,
@@ -127,44 +129,59 @@
 
     normed_ref[...] = rms_scale(hidden_ref[...], gain_ref[...]).astype(bf16)
     normed = normed_ref[...]
-    dt_in = dot(normed, w_dt_ref[...]).astype(bf16)
+    dt_in = dot_rows(normed, w_dt_ref[...]).astype(bf16)
     loads[0].wait()
     ssm_in = dot(normed, w_x[...]).astype(bf16)
     loads[1].wait()
     bc_in = dot(normed, w_bc[...]).astype(bf16)
 
-    row_at = lax.broadcasted_iota(jnp.int32, (1, rows_x_ref.shape[0]), 1)
-    rows_x, rows_bc = rows_x_ref[...], rows_bc_ref[...]
+    def starting(rows_ref):
+        rows = rows_ref[...].astype(f32)
+        return [
+            jnp.where(first_prompt, rows[i, 0:1], rows[i, 1:2]) for i in range(edge)
+        ]
+
     keep = position < edge
     kept_at = accepted + position
     pick_drafts = ones_where(same & keep & (other_position == kept_at - edge))
-    pick_prompt = ones_where((row_at == member * edge + kept_at) & (kept_at < edge) & keep)
-    edge_x_ref[...] = (dot(pick_drafts, ssm_in) + dot(pick_prompt, rows_x)).astype(bf16)
-    edge_bc_ref[...] = (dot(pick_drafts, bc_in) + dot(pick_prompt, rows_bc)).astype(bf16)
-
-    def convolved(series, rows, taps):
+
+    def kept_rows(series, start):
+        kept = dot(pick_drafts, series)
+        for i in range(edge):
+            kept = jnp.where(keep & (kept_at == i), start[i], kept)
+        return kept.astype(bf16)
+
+    start_x, start_bc = starting(rows_x_ref), starting(rows_bc_ref)
+    edge_x_ref[...] = kept_rows(ssm_in, start_x)
+    edge_bc_ref[...] = kept_rows(bc_in, start_bc)
+
+    def convolved(series, start, taps):
         wide = series.astype(f32)
         total = wide * taps[edge : edge + 1].astype(f32)
         for back in range(1, CONV):
-            shifted = jnp.where(position >= back, pltpu.roll(wide, back, 0), 0.0)
-            begin = ones_where(
-                (row_at == member * edge + edge + position - back) & (position < back)
-            )
-            shifted = shifted + dot(begin, rows)
+            shifted = pltpu.roll(wide, back, 0)
+            for at in range(back):
+                shifted = jnp.where(position == at, start[edge + at - back], shifted)
             total = total + shifted * taps[edge - back : edge - back + 1].astype(f32)
         return jax.nn.silu(total)
 
-    x = convolved(ssm_in, rows_x, conv_x_ref[...])
-    bc = convolved(bc_in, rows_bc, conv_bc_ref[...])
+    x = convolved(ssm_in, start_x, conv_x_ref[...])
+    bc = convolved(bc_in, start_bc, conv_bc_ref[...])
     b_part = bc[:, :STATE].astype(bf16)
     c_part = bc[:, STATE:].astype(bf16)
 
     head_row = lax.broadcasted_iota(jnp.int32, (dt_in.shape[1], inner), 0)
     head_col = lax.broadcasted_iota(jnp.int32, (dt_in.shape[1], inner), 1)
     spread = ones_where(head_row == head_col // SSM_DIM)
-    dt_bias = head_params_ref[0:1, :]
-    rate = head_params_ref[1:2, :]
-    skip = head_params_ref[2:3, :]
+    head_at = lax.broadcasted_iota(jnp.int32, (1, inner), 1) // SSM_DIM
+
+    def per_channel(ref):
+        values = jnp.zeros((1, inner), f32)
+        for h in range(heads):
+            values = jnp.where(head_at == h, ref[h], values)
+        return values
+
+    dt_bias, rate, skip = per_channel(dt_bias_ref), per_channel(rate_ref), per_channel(skip_ref)
     raw = dot(dt_in, spread) + dt_bias
     step_size = jnp.maximum(raw, 0.0) + jnp.log1p(jnp.exp(-jnp.abs(raw)))
     log_decay = dot_exact(ones_where(causal, f32), -step_size * rate)
@@ -255,7 +272,9 @@
     conv_bc,
     rows_x,
     rows_bc,
-    head_params,
+    dt_bias,
+    ssm_rate,
+    skip_d,
     w_query,
     w_kv,
     prompt_kv,
@@ -281,7 +300,7 @@
             jax.ShapeDtypeStruct((tokens, w_x.shape[1]), bf16),
             jax.ShapeDtypeStruct((tokens, w_bc.shape[1]), bf16),
         ),
-        in_specs=[smem] * 3 + [vmem] * 8 + [anywhere] * 9,
+        in_specs=[smem] * 3 + [vmem] * 7 + [smem] * 3 + [anywhere] * 9,
         out_specs=(vmem,) * 4,
         scratch_shapes=[
             pltpu.VMEM(w_query.shape, bf16),
@@ -296,7 +315,7 @@
             pltpu.VMEM((tokens, width), bf16),
             pltpu.SemaphoreType.DMA((9,)),
         ],
-        compiler_params=pltpu.CompilerParams(vmem_limit_bytes=40 * 1024 * 1024),
+        compiler_params=pltpu.CompilerParams(vmem_limit_bytes=63 * 1024 * 1024),
     )(
         member,
         lengths,
@@ -308,7 +327,9 @@
         conv_bc,
         rows_x,
         rows_bc,
-        head_params,
+        dt_bias,
+        ssm_rate,
+        skip_d,
         w_query,
         w_kv,
         prompt_kv,
@@ -334,11 +355,13 @@
     down_hbm,
     head_hbm,
     kept_hbm,
-    edge_hbm,
+    edge_ref,
+    edge_bc_ref,
     hidden_out_ref,
     verify_ref,
     kept_out,
-    edge_out,
+    kept_conv_ref,
+    edge_in,
     gate_w,
     up_w,
     down_w,
@@ -423,6 +446,35 @@
     total = mixed_ref[pl.ds(mdl * block, block)].astype(jnp.float32)
     for copy in mixes:
         copy.wait_recv()
+    moves = []
+    for d in range(1, m):
+        to = (mdl + d) % m
+        moves.append(
+            send(
+                kept_hbm.at[pl.ds(to * own_reqs, own_reqs)],
+                kept_out.at[:, pl.ds(mdl * heads, heads)],
+                kept_sems,
+                d - 1,
+                (req, to),
+            )
+        )
+        moves.append(
+            send(
+                edge_ref.at[pl.ds(to * own_reqs, own_reqs)],
+                edge_in.at[mdl],
+                edge_sems,
+                d - 1,
+                (req, to),
+            )
+        )
+    own_kept = pltpu.make_async_copy(
+        kept_hbm.at[pl.ds(mdl * own_reqs, own_reqs)],
+        kept_out.at[:, pl.ds(mdl * heads, heads)],
+        load_sems.at[4],
+    )
+    own_kept.start()
+    edge_in[mdl] = edge_ref[pl.ds(mdl * own_reqs, own_reqs)]
+
     for d in range(m - 1):
         total = total + mix_in[d].astype(jnp.float32)
     after = (
@@ -448,38 +500,6 @@
         return sent + across
 
     waits = gather_rows(rows_ref, gather_sems)
-
-    moves = []
-    for d in range(1, m):
-        to = (mdl + d) % m
-        moves.append(
-            send(
-                kept_hbm.at[pl.ds(to * own_reqs, own_reqs)],
-                kept_out.at[:, pl.ds(mdl * heads, heads)],
-                kept_sems,
-                d - 1,
-                (req, to),
-            )
-        )
-        moves.append(
-            send(
-                edge_hbm.at[pl.ds(to * own_reqs, own_reqs)],
-                edge_out.at[mdl],
-                edge_sems,
-                d - 1,
-                (req, to),
-            )
-        )
-    own_kept = pltpu.make_async_copy(
-        kept_hbm.at[pl.ds(mdl * own_reqs, own_reqs)],
-        kept_out.at[:, pl.ds(mdl * heads, heads)],
-        load_sems.at[4],
-    )
-    own_edge = pltpu.make_async_copy(
-        edge_hbm.at[pl.ds(mdl * own_reqs, own_reqs)], edge_out.at[mdl], load_sems.at[5]
-    )
-    own_kept.start()
-    own_edge.start()
 
     for load in loads[:3]:
         load.wait()
@@ -548,7 +568,18 @@
     loads[3].wait()
     vocab_here = head_w.shape[0]
     vocab_step = 512
-    ids = ids_ref[0:1, :]
+    at_token = lax.broadcasted_iota(jnp.int32, (ids_ref.shape[1], tokens), 1)
+    at_request = lax.broadcasted_iota(jnp.int32, (ids_ref.shape[1], tokens), 0)
+    own_request = (
+        at_token // block * (own_reqs * m) + mdl * own_reqs + at_token % block // DRAFT
+    )
+    spread = jnp.where(at_request == own_request, 1.0, 0.0)
+    by_draft = dot_exact(ids_ref[...].astype(jnp.float32), spread)
+    at_draft = lax.broadcasted_iota(jnp.int32, (DRAFT, tokens), 0)
+    next_draft = (lax.broadcasted_iota(jnp.int32, (DRAFT, tokens), 1) + 1) % DRAFT
+    ids = jnp.sum(
+        jnp.where(at_draft == next_draft, by_draft, 0.0), axis=0, keepdims=True
+    )
     start = (
         jnp.full((1, tokens), far_below, jnp.float32),
         jnp.zeros((1, tokens), jnp.float32),
@@ -565,7 +596,7 @@
             req * vocab_here + first + lax.broadcasted_iota(jnp.int32, (vocab_step, tokens), 0)
         )
         target = target + jnp.sum(
-            jnp.where(vocab_ids == ids, logits, 0.0), axis=0, keepdims=True
+            jnp.where(vocab_ids.astype(jnp.float32) == ids, logits, 0.0), axis=0, keepdims=True
         )
         new_top = jnp.maximum(top, jnp.max(logits, axis=0, keepdims=True))
         weight = weight * jnp.exp(top - new_top) + jnp.sum(
@@ -590,18 +621,42 @@
     target = jnp.sum(targets, axis=0)
     position = lax.broadcasted_iota(jnp.int32, (1, tokens), 1) % DRAFT
     score = jnp.where(position < DRAFT - 1, target, top) - log_total
-    verify_ref[...] = jnp.broadcast_to(score, verify_ref.shape)
+    scores = jnp.broadcast_to(score, (8, tokens))
+    from_token = lax.broadcasted_iota(jnp.int32, (tokens, DRAFT), 0)
+    to_draft = lax.broadcasted_iota(jnp.int32, (tokens, DRAFT), 1)
+    verify_ref[...] = jnp.concatenate(
+        [
+            dot_exact(
+                scores,
+                jnp.where(from_token == req * block + r * DRAFT + to_draft, 1.0, 0.0),
+            )[0:1]
+            for r in range(own_reqs)
+        ],
+        axis=0,
+    )
 
     for copy in mixes + waits + shares:
         copy.wait_send()
     for copy in moves:
         copy.wait()
     own_kept.wait()
-    own_edge.wait()
+
+    def edge_rows(j, k):
+        rows = [edge_in[j, r].astype(jnp.float32)[k : k + 1] for r in range(own_reqs)]
+        return jnp.concatenate(rows, axis=0)
+
+    for k in range(CONV - 1):
+        bc_rows = [
+            edge_bc_ref[mdl * own_reqs + r].astype(jnp.float32)[k : k + 1]
+            for r in range(own_reqs)
+        ]
+        kept_conv_ref[k] = jnp.concatenate(
+            [edge_rows(j, k) for j in range(m)] + [jnp.concatenate(bc_rows, axis=0)], axis=1
+        ).astype(jnp.bfloat16)
 
 
 def run_tail(
-    mixed, hidden, mlp_gain, final_gain, ids, w_gate, w_up, w_down, head_weight, kept, edges
+    mixed, hidden, mlp_gain, final_gain, ids, w_gate, w_up, w_down, head_weight, kept, edges, edges_bc
 ):
     n = lax.axis_size("req")
     m = lax.axis_size("mdl")
@@ -619,13 +674,16 @@
         functools.partial(tail_kernel, n, m),
         out_shape=(
             jax.ShapeDtypeStruct((block, width), bf16),
-            jax.ShapeDtypeStruct((8, tokens), jnp.float32),
+            jax.ShapeDtypeStruct((own_reqs, DRAFT), jnp.float32),
             jax.ShapeDtypeStruct((own_reqs, heads * m) + kept.shape[2:], bf16),
-            jax.ShapeDtypeStruct((m, own_reqs) + edges.shape[1:], bf16),
+            jax.ShapeDtypeStruct(
+                (CONV - 1, own_reqs, m * edges.shape[2] + edges_bc.shape[2]), bf16
+            ),
         ),
-        in_specs=[vmem] * 5 + [anywhere] * 6,
-        out_specs=(vmem, vmem, anywhere, anywhere),
+        in_specs=[vmem] * 5 + [anywhere] * 5 + [vmem] * 2,
+        out_specs=(vmem, vmem, anywhere, vmem),
         scratch_shapes=[
+            pltpu.VMEM((m, own_reqs) + edges.shape[1:], bf16),
             pltpu.VMEM(w_gate.shape, bf16),
             pltpu.VMEM(w_up.shape, bf16),
             pltpu.VMEM(w_down.shape, bf16),
@@ -641,7 +699,7 @@
             pltpu.VMEM((chips - 1, block, width), bf16),
             pltpu.VMEM((chips - 1, block, width), bf16),
             pltpu.VMEM((n, 8, tokens), jnp.float32),
-            sems((6,)),
+            sems((5,)),
             sems((2, m - 1)),
             sems((2, 2 * chips - 1)),
             sems((2, 2 * chips - 1)),
@@ -652,9 +710,11 @@
             sems((2, m - 1)),
         ],
         compiler_params=pltpu.CompilerParams(
-            collective_id=0, has_side_effects=True, vmem_limit_bytes=50 * 1024 * 1024
+            collective_id=0, has_side_effects=True, vmem_limit_bytes=63 * 1024 * 1024
         ),
-    )(mixed, hidden, mlp_gain, final_gain, ids, w_gate, w_up, w_down, head_weight, kept, edges)
+    )(
+        mixed, hidden, mlp_gain, final_gain, ids, w_gate, w_up, w_down, head_weight, kept, edges, edges_bc
+    )
 
 
 def shards(
@@ -689,33 +749,23 @@
     draft_ids,
 ):
     row_reqs, draft_len, width = hidden_in.shape
-    mdl_count = lax.axis_size("mdl")
-    req_count = lax.axis_size("req")
-    mdl_rank = lax.axis_index("mdl")
-    req_rank = lax.axis_index("req")
-    row_tokens = row_reqs * draft_len
-    own_reqs = row_reqs // mdl_count
-    own_tokens = own_reqs * draft_len
-    flat_rows = hidden_in.reshape(row_tokens, width)
-    edge_len = CONV - 1
+    own_reqs = row_reqs // lax.axis_size("mdl")
     local_inner = w_x.shape[1]
-
-    def edge_rows(rows):
-        rows = rows.reshape(PROMPTS * edge_len, rows.shape[2])
-        return jnp.pad(rows, ((0, 16 - PROMPTS * edge_len), (0, 0)))
-
+    flat_rows = hidden_in.reshape(row_reqs * draft_len, width)
     mixed, kept_states, edge_x_rows, edge_bc_rows = run_mixers(
         member,
         prompt_lengths,
         accepted,
         flat_rows,
-        mixer_gain.reshape(1, width),
-        w_dt,
+        mixer_gain,
+        w_dt.T,
         conv_x,
         conv_bc,
-        edge_rows(prompt_conv_x),
-        edge_rows(prompt_conv_bc),
-        jnp.repeat(jnp.stack([dt_bias, ssm_rate, skip_d]), SSM_DIM, axis=1),
+        prompt_conv_x.transpose(1, 0, 2),
+        prompt_conv_bc.transpose(1, 0, 2),
+        dt_bias,
+        ssm_rate,
+        skip_d,
         w_query,
         w_kv,
         prompt_kv,
@@ -726,36 +776,26 @@
         w_attn_out,
         w_mamba_out,
     )
-    edges = edge_x_rows.reshape(row_reqs, draft_len, local_inner)
-    kept_bc = edge_bc_rows.reshape(row_reqs, draft_len, 2 * STATE)[:, :edge_len]
-    id_grid = draft_ids.reshape(req_count, mdl_count, own_reqs, draft_len)
-    column_ids = lax.dynamic_index_in_dim(id_grid, mdl_rank, 1, keepdims=False)
-    next_ids = jnp.concatenate([column_ids[..., 1:], column_ids[..., :1]], axis=-1).reshape(1, -1)
-    hidden_out, scores_all, kept_all, edges_all = run_tail(
+    hidden_out, verify_scores, kept_all, kept_conv = run_tail(
         mixed,
         flat_rows,
-        mlp_gain.reshape(1, width),
-        final_gain.reshape(1, width),
-        jnp.broadcast_to(next_ids, (8, next_ids.shape[1])),
+        mlp_gain,
+        final_gain,
+        draft_ids.T,
         w_gate,
         w_up,
         w_down,
         head_weight,
         kept_states,
-        edges,
-    )
-    kept_state = kept_all.astype(jnp.float32)
-    edge_x = (
-        edges_all[:, :, :edge_len]
-        .transpose(1, 2, 0, 3)
-        .reshape(own_reqs, edge_len, mdl_count * local_inner)
-    )
-    own_bc = lax.dynamic_slice_in_dim(kept_bc, mdl_rank * own_reqs, own_reqs, 0)
-    kept_conv = jnp.concatenate([edge_x, own_bc], axis=2)
-    verify_scores = lax.dynamic_slice_in_dim(
-        scores_all[0], req_rank * own_tokens, own_tokens, 0
-    ).reshape(own_reqs, draft_len)
-    return (hidden_out.reshape(own_reqs, draft_len, width), verify_scores, kept_state, kept_conv)
+        edge_x_rows.reshape(row_reqs, draft_len, local_inner),
+        edge_bc_rows.reshape(row_reqs, draft_len, 2 * STATE),
+    )
+    return (
+        hidden_out.reshape(own_reqs, draft_len, width),
+        verify_scores,
+        kept_all.astype(jnp.float32),
+        kept_conv.transpose(1, 0, 2),
+    )
 
 
 def solution(mesh):

time: 98.3 us -> 75.6 us (0.77); the launches traced: 96.8 us -> 75.4 us
  local copies, waits for them, and re-layouts: 22.1 us -> 1.84 us
  Pallas kernels: 70.5 us -> 69.4 us
    unnamed x36 -> x9, local copies, waits for them, and re-layouts: 18.8 us -> 1.84 us
    pallas_call x1, Pallas kernels: 62.1 us -> 59.2 us  [run_tail(): pl.pallas_call(functools.partial(tail_kernel, n, m), out_shape=(jax.Shape...]
    reshape x8 -> x0, local copies, waits for them, and re-layouts: 2.86 us -> none  [the longest x1 0.69 us: shards(): mixer_gain.reshape(1, width)]
    pallas_call x1, Pallas kernels: 8.36 us -> 10.2 us  [run_mixers(): pl.pallas_call(functools.partial(mixer_kernel, m), out_shape=(jax.ShapeDt...]
    convert_element_type x1, other arithmetic: 2.06 us -> 3.52 us  [shards(): kept_all.astype(jnp.float32)]
where the time goes in v3:
time: 75.6 us; the launch traced here: 75.4 us
  Pallas kernels  69.4 us (92%)
  other arithmetic  3.52 us (5%)
  local copies, waits for them, and re-layouts  1.84 us (2%)
    pallas_call x1, Pallas kernels, run_tail(): pl.pallas_call(functools.partial(tail_kernel, n, m), out_shape=(jax.Shape...  59.2 us
    pallas_call x1, Pallas kernels, run_mixers(): pl.pallas_call(functools.partial(mixer_kernel, m), out_shape=(jax.ShapeDt...  10.2 us
    convert_element_type x1, other arithmetic, shards(): kept_all.astype(jnp.float32)  3.52 us
    unnamed x9, local copies, waits for them, and re-layouts  1.84 us

profile of v3, /device:TPU:9, one launch (start us, length us, event | category | flops | bytes accessed | tf_op | source)
XLA Modules:
  0.0 75.4 jit_solution(12992356448755386334)
XLA Ops:
  0.6 10.2 %shard_map.300 = (bf16[128,2048]{1,0:T(8,128)(2,1)}, bf16[8,6,64,256]{3,2,1,0:T(8,128)(2,1)}, bf16[128,384]{1,0:T(8,128)(2,1)}, bf16[128,512]{1,0:T(8,128)(2,1)}) custom-call(s32[8]{0:T(128)} %member_ref.1, s32[2]{0:T(128)} %lengths_ref.1, s32[8]{0:T(128)} %accepted_ref.1, bf16[128,2048]{1,0:T(8,128)(2,1)} %bitcast.9, bf16[2048]{0:T(1024)(128)(2,1)} %gain_ref.1, ...), custom_call_target="tpu_custom_call" | custom-call | tf_op jit(solution)/shard_map/pallas_call | solution.py:295
  10.8 59.2 %shard_map.301 = (bf16[32,2048]{1,0:T(8,128)(2,1)}, f32[2,16]{1,0:T(2,128)}, bf16[2,24,64,256]{3,2,1,0:T(8,128)(2,1)}, bf16[3,2,2048]{2,1,0:T(2,128)(2,1)}) custom-call(bf16[128,2048]{1,0:T(8,128)(2,1)} %get-tuple-element.12.mixed_ref, bf16[128,2048]{1,0:T(8,128)(2,1)} %bitcast.10, bf16[2048]{0:T(1024)(128)(2,1)} %mlp_gain_ref.1, ...), custom_call_target="tpu_custom_call" | custom-call | tf_op jit(solution)/shard_map/pallas_call | solution.py:673
  70.0 0.0 copy-start
  70.1 0.0 copy-start.2
  70.1 0.0 copy-start.1
  70.1 3.5 %convert_element_type.3 = f32[2,24,64,256]{3,2,1,0:T(8,128)} convert(bf16[2,24,64,256]{3,2,1,0:T(8,128)(2,1)} %get-tuple-element.18) | non-fusion elementwise | flops 786432 | bytes 4718592 | tf_op jit(solution)/shard_map/convert_element_type | solution.py:796
  73.6 0.0 copy-done
  73.6 0.7 copy.36
  74.3 0.0 copy-done.2
  74.3 0.6 copy.37
  74.8 0.0 copy-done.1
  74.8 0.6 copy.38
Async XLA Ops:
  70.0 3.6 %copy-start = (bf16[32,2048]{1,0:T(8,128)(2,1)S(1)}, bf16[32,2048]{1,0:T(8,128)(2,1)}, u32[]{:S(2)}) copy-start(bf16[32,2048]{1,0:T(8,128)(2,1)} %get-tuple-element.16) | copy-start | bytes 393220
  70.1 4.2 %copy-start.2 = (f32[2,16]{1,0:T(2,128)S(1)}, f32[2,16]{1,0:T(2,128)}, u32[]{:S(2)}) copy-start(f32[2,16]{1,0:T(2,128)} %get-tuple-element.25) | copy-start | bytes 388
  70.1 4.8 %copy-start.1 = (bf16[3,2,2048]{2,1,0:T(2,128)(2,1)S(1)}, bf16[3,2,2048]{2,1,0:T(2,128)(2,1)}, u32[]{:S(2)}) copy-start(bf16[3,2,2048]{2,1,0:T(2,128)(2,1)} %get-tuple-element.19) | copy-start | bytes 73732

commit v4 on v3

--- a/solution.py
+++ b/solution.py
@@ -513,14 +513,14 @@
         first = part * group
         prepared = rows_ref[pl.ds(first, group)].reshape(256, width)
 
-        @pl.loop(0, units // unit_step)
+        @pl.loop(0, units // unit_step, unroll=units // unit_step)
         def _(step):
             at = pl.ds(pl.multiple_of(step * unit_step, unit_step), unit_step)
             gate_val = jnp.dot(prepared, gate_w[:, at], preferred_element_type=jnp.float32)
             up_val = jnp.dot(prepared, up_w[:, at], preferred_element_type=jnp.float32)
             active_ref[:, at] = (jax.nn.silu(gate_val) * up_val).astype(jnp.bfloat16)
 
-        @pl.loop(0, width // column_step)
+        @pl.loop(0, width // column_step, unroll=2)
         def _(step):
             at = pl.ds(pl.multiple_of(step * column_step, column_step), column_step)
             value = jnp.dot(active_ref[...], down_w[:, at], preferred_element_type=jnp.float32)
@@ -558,7 +558,7 @@
     waits += pairs
     waits += gather_rows(final_ref, final_sems)
 
-    @pl.loop(0, width // 256)
+    @pl.loop(0, width // 256, unroll=4)
     def _(step):
         at = pl.ds(pl.multiple_of(step * 256, 256), 256)
         final_t[at, :] = (
@@ -604,7 +604,9 @@
         )
         return (new_top, weight, target)
 
-    top, weight, target = lax.fori_loop(0, vocab_here // vocab_step, head_step, start)
+    top, weight, target = lax.fori_loop(
+        0, vocab_here // vocab_step, head_step, start, unroll=min(4, vocab_here // vocab_step)
+    )
     stats_ref[req] = jnp.concatenate(
         [top, weight, target, jnp.zeros((5, tokens), jnp.float32)], axis=0
     )

time: 75.6 us -> 73.6 us (0.974)
  Pallas kernels: 69.4 us -> 67.4 us
    pallas_call x1, Pallas kernels: 59.2 us -> 57.2 us  [run_tail(): pl.pallas_call(functools.partial(tail_kernel, n, m), out_shape=(jax.Shape...]
where the time goes in v4:
time: 73.6 us; the launch traced here: 73.4 us
  Pallas kernels  67.4 us (92%)
  other arithmetic  3.52 us (5%)
  local copies, waits for them, and re-layouts  1.84 us (2%)
    pallas_call x1, Pallas kernels, run_tail(): pl.pallas_call(functools.partial(tail_kernel, n, m), out_shape=(jax.Shape...  57.2 us
    pallas_call x1, Pallas kernels, run_mixers(): pl.pallas_call(functools.partial(mixer_kernel, m), out_shape=(jax.ShapeDt...  10.2 us
    convert_element_type x1, other arithmetic, shards(): kept_all.astype(jnp.float32)  3.52 us
    unnamed x9, local copies, waits for them, and re-layouts  1.84 us

profile of v4, /device:TPU:9, one launch (start us, length us, event | category | flops | bytes accessed | tf_op | source)
XLA Modules:
  0.0 73.4 jit_solution(10792785666848442643)
XLA Ops:
  0.6 10.2 %shard_map.300 = (bf16[128,2048]{1,0:T(8,128)(2,1)}, bf16[8,6,64,256]{3,2,1,0:T(8,128)(2,1)}, bf16[128,384]{1,0:T(8,128)(2,1)}, bf16[128,512]{1,0:T(8,128)(2,1)}) custom-call(s32[8]{0:T(128)} %member_ref.1, s32[2]{0:T(128)} %lengths_ref.1, s32[8]{0:T(128)} %accepted_ref.1, bf16[128,2048]{1,0:T(8,128)(2,1)} %bitcast.9, bf16[2048]{0:T(1024)(128)(2,1)} %gain_ref.1, ...), custom_call_target="tpu_custom_call" | custom-call | tf_op jit(solution)/shard_map/pallas_call | solution.py:295
  10.8 57.2 %shard_map.301 = (bf16[32,2048]{1,0:T(8,128)(2,1)}, f32[2,16]{1,0:T(2,128)}, bf16[2,24,64,256]{3,2,1,0:T(8,128)(2,1)}, bf16[3,2,2048]{2,1,0:T(2,128)(2,1)}) custom-call(bf16[128,2048]{1,0:T(8,128)(2,1)} %get-tuple-element.12.mixed_ref, bf16[128,2048]{1,0:T(8,128)(2,1)} %bitcast.10, bf16[2048]{0:T(1024)(128)(2,1)} %mlp_gain_ref.1, ...), custom_call_target="tpu_custom_call" | custom-call | tf_op jit(solution)/shard_map/pallas_call | solution.py:675
  68.1 0.0 copy-start
  68.1 0.0 copy-start.2
  68.1 0.0 copy-start.1
  68.1 3.5 %convert_element_type.3 = f32[2,24,64,256]{3,2,1,0:T(8,128)} convert(bf16[2,24,64,256]{3,2,1,0:T(8,128)(2,1)} %get-tuple-element.18) | non-fusion elementwise | flops 786432 | bytes 4718592 | tf_op jit(solution)/shard_map/convert_element_type | solution.py:798
  71.6 0.0 copy-done
  71.6 0.7 copy.36
  72.3 0.0 copy-done.2
  72.3 0.6 copy.37
  72.8 0.0 copy-done.1
  72.8 0.6 copy.38
Async XLA Ops:
  68.1 3.6 %copy-start = (bf16[32,2048]{1,0:T(8,128)(2,1)S(1)}, bf16[32,2048]{1,0:T(8,128)(2,1)}, u32[]{:S(2)}) copy-start(bf16[32,2048]{1,0:T(8,128)(2,1)} %get-tuple-element.16) | copy-start | bytes 393220
  68.1 4.2 %copy-start.2 = (f32[2,16]{1,0:T(2,128)S(1)}, f32[2,16]{1,0:T(2,128)}, u32[]{:S(2)}) copy-start(f32[2,16]{1,0:T(2,128)} %get-tuple-element.25) | copy-start | bytes 388
  68.1 4.8 %copy-start.1 = (bf16[3,2,2048]{2,1,0:T(2,128)(2,1)S(1)}, bf16[3,2,2048]{2,1,0:T(2,128)(2,1)}, u32[]{:S(2)}) copy-start(bf16[3,2,2048]{2,1,0:T(2,128)(2,1)} %get-tuple-element.19) | copy-start | bytes 73732
